TPU v7x, 32 devices: a whole 2x2x4 slice. The times are simulated.
32 devices in a mesh: dp: 8 (over y, x, core), ffn: 4 (over z).
Axes of the slice: x: 2, y: 2, z: 4, core: 2. Of those that a mesh axis runs over, the one named last changes fastest.
Arguments:
- tokens: bfloat16 [49152, 768], P(('dp', 'ffn')), may hold values from -6 to 6
- lengths: int32 [96], P(('dp', 'ffn')), may hold values from 32 to 512, as said below
- qkv_weight: bfloat16 [2304, 192], P(('dp', 'ffn')), may hold values from -0.4375 to 0.4375
- out_weight: bfloat16 [768, 768], P(('dp', 'ffn')), may hold values from -0.875 to 0.875
- ffn_in_weight: bfloat16 [4, 192, 768], P(None, 'dp', 'ffn'), may hold values from -0.4375 to 0.4375
- ffn_out_weight: bfloat16 [4, 768, 192], P(None, 'ffn', 'dp'), may hold values from -0.21875 to 0.21875
- biases: bfloat16 [10, 768], P(None, ('dp', 'ffn')), may hold values from -3 to 3
- gains: bfloat16 [2, 768], P(None, ('dp', 'ffn')), may hold values from 0.5 to 1.5
- cotangent: bfloat16 [49152, 768], P(('dp', 'ffn')), may hold values from -6 to 6
Outputs:
- output: bfloat16 [49152, 768], P(('dp', 'ffn'))
- grad_tokens: bfloat16 [49152, 768], P(('dp', 'ffn'))
- grad_qkv_weight: float32 [2304, 192], P(('dp', 'ffn'))
- grad_out_weight: float32 [768, 768], P(('dp', 'ffn'))
- grad_ffn_in_weight: float32 [4, 192, 768], P(None, 'dp', 'ffn')
- grad_ffn_out_weight: float32 [4, 768, 192], P(None, 'ffn', 'dp')
- grad_biases: float32 [10, 768], P(None, ('dp', 'ffn'))
- grad_gains: float32 [2, 768], P(None, ('dp', 'ffn'))
Inputs may be any that keep to these rules, and one draw needn't show every extreme that they name: `lengths`: one slot of the whole batch holds a sequence of the full 512 positions.
All inputs are finite; a program needn't handle non-finite values.
Results may differ from a plain program's by a relative error of at most 0.017.
Values may be sent and summed in bfloat16 or wider, within the bound.
A program may use at most 320 MiB of HBM per device.

v0:
```python
import jax
import jax.numpy as jnp
from jax import lax
from jax.sharding import PartitionSpec as P

HEADS = 12
GROUPS = 4


EPSILON = 1e-12
NEGATIVE = -1e30


def grouped(values, weight):
    count = values.shape[0]
    split = values.reshape(count, weight.shape[0], weight.shape[1])
    return jnp.einsum("ngi,gio->ngo", split, weight, preferred_element_type=jnp.float32).reshape(
        count, -1
    )


def grouped_back(gradient, weight):
    count = gradient.shape[0]
    split = gradient.reshape(count, weight.shape[0], weight.shape[2])
    return jnp.einsum("ngo,gio->ngi", split, weight, preferred_element_type=jnp.float32).reshape(
        count, -1
    )


def grouped_weight(values, gradient, group_count):
    count = values.shape[0]
    return jnp.einsum(
        "ngi,ngo->gio",
        values.reshape(count, group_count, -1),
        gradient.reshape(count, group_count, -1),
        preferred_element_type=jnp.float32,
    )


def normalize(residual, gain_row, offset_row):
    centre = residual - jnp.mean(residual, axis=-1, keepdims=True)
    inverse = lax.rsqrt(jnp.mean(centre * centre, axis=-1, keepdims=True) + EPSILON)
    normed = centre * inverse
    return (normed * gain_row + offset_row, normed, inverse)


def normalize_back(upstream, normed, inverse, gain_row):
    inner = upstream * gain_row
    mean_inner = jnp.mean(inner, axis=-1, keepdims=True)
    mean_cross = jnp.mean(inner * normed, axis=-1, keepdims=True)
    grad_residual = inverse * (inner - mean_inner - normed * mean_cross)
    return (grad_residual, jnp.sum(upstream * normed, axis=0), jnp.sum(upstream, axis=0))


def gelu_pair(pre_act):
    cumulative = 0.5 * (1.0 + jax.scipy.special.erf(pre_act * 0.7071067811865476))
    density = jnp.exp(-0.5 * pre_act * pre_act) * 0.3989422804014327
    return (pre_act * cumulative, cumulative + pre_act * density)


def on_device(
    tokens, lengths, qkv_weight, out_weight, ffn_in_weight, ffn_out_weight, biases, gains, cotangent
):
    row_count, model_width = tokens.shape
    slot_count = lengths.shape[0]
    slot_rows = row_count // slot_count
    head_size = model_width // HEADS
    group_width = model_width // GROUPS
    score_scale = head_size ** (-0.5)
    qkv_all, out_all, bias_all, gain_all = (
        lax.all_gather(qkv_weight, ("dp", "ffn"), axis=0, tiled=True),
        lax.all_gather(out_weight, ("dp", "ffn"), axis=0, tiled=True),
        lax.all_gather(biases, ("dp", "ffn"), axis=1, tiled=True),
        lax.all_gather(gains, ("dp", "ffn"), axis=1, tiled=True),
    )
    projections = qkv_all.reshape(3, GROUPS, group_width, group_width)
    bias_rows = bias_all.astype(jnp.float32)
    gain_rows = gain_all.astype(jnp.float32)
    inputs = tokens.astype(jnp.float32)
    query = (grouped(tokens, projections[0]) + bias_rows[GROUPS]).astype(jnp.bfloat16)
    keys = grouped(tokens, projections[1]).astype(jnp.bfloat16)
    values = (grouped(tokens, projections[2]) + bias_rows[GROUPS + 1]).astype(jnp.bfloat16)
    positions = jnp.arange(slot_rows)

    def split_heads(array):
        return array.reshape(slot_count, slot_rows, HEADS, head_size)

    def slot_scores(query_slot, key_slot, length):
        raw_scores = (
            jnp.einsum("qhd,khd->hqk", query_slot, key_slot, preferred_element_type=jnp.float32)
            * score_scale
        )
        return jnp.where((positions < length)[None, None, :], raw_scores, NEGATIVE)

    def attend(packed):
        query_slot, key_slot, value_slot, length = packed
        logits = slot_scores(query_slot, key_slot, length)
        row_max = jnp.max(logits, axis=-1, keepdims=True)
        exponent = jnp.exp(logits - row_max)
        row_total = jnp.sum(exponent, axis=-1, keepdims=True)
        probabilities = (exponent / row_total).astype(jnp.bfloat16)
        mixed = jnp.einsum(
            "hqk,khd->qhd", probabilities, value_slot, preferred_element_type=jnp.float32
        )
        return (
            mixed.reshape(slot_rows, model_width).astype(jnp.bfloat16),
            (row_max + jnp.log(row_total))[..., 0],
        )

    context, log_totals = lax.map(
        attend, (split_heads(query), split_heads(keys), split_heads(values), lengths)
    )
    context = context.reshape(row_count, model_width)
    attn_out = jnp.dot(context, out_all, preferred_element_type=jnp.float32) + bias_rows[GROUPS + 2]
    first_norm, normed_first, inverse_first = normalize(
        inputs + attn_out, gain_rows[0], bias_rows[GROUPS + 3]
    )
    first_low = first_norm.astype(jnp.bfloat16)
    ffn_place = lax.axis_index("ffn")
    ffn_count = lax.axis_size("ffn")
    w_in, w_out = (
        lax.all_gather(ffn_in_weight, "dp", axis=1, tiled=True),
        lax.all_gather(ffn_out_weight, "dp", axis=2, tiled=True),
    )
    local_units = w_in.shape[2]
    inner_bias = lax.dynamic_slice_in_dim(
        bias_rows[:GROUPS], ffn_place * local_units, local_units, 1
    ).reshape(-1)
    gathered = lax.all_gather(first_low, "ffn", axis=0, tiled=True)
    pre_act = grouped(gathered, w_in) + inner_bias
    activation, gelu_slope = gelu_pair(pre_act)
    act_low = activation.astype(jnp.bfloat16)
    ffn_branch = lax.psum_scatter(
        grouped(act_low, w_out).astype(jnp.bfloat16), "ffn", scatter_dimension=0, tiled=True
    ).astype(jnp.float32)
    second_norm, normed_second, inverse_second = normalize(
        first_norm + ffn_branch + bias_rows[GROUPS + 4], gain_rows[1], bias_rows[GROUPS + 5]
    )
    upstream = cotangent.astype(jnp.float32)
    grad_second, grad_gain_second, grad_shift_second = normalize_back(
        upstream, normed_second, inverse_second, gain_rows[1]
    )
    grad_branch = grad_second.astype(jnp.bfloat16)
    grad_out_bias_ffn = jnp.sum(grad_branch, axis=0, dtype=jnp.float32)
    grad_gathered = lax.all_gather(grad_branch, "ffn", axis=0, tiled=True)
    grad_pre = (grouped_back(grad_gathered, w_out) * gelu_slope).astype(jnp.bfloat16)
    grad_w_in = grouped_weight(gathered, grad_pre, GROUPS)
    grad_w_out = grouped_weight(act_low, grad_gathered, GROUPS)
    grad_first_branch = lax.psum_scatter(
        grouped_back(grad_pre, w_in).astype(jnp.bfloat16), "ffn", scatter_dimension=0, tiled=True
    ).astype(jnp.float32)
    local_bias = jnp.sum(grad_pre, axis=0, dtype=jnp.float32).reshape(GROUPS, local_units)
    grad_inner_bias = lax.dynamic_update_slice_in_dim(
        jnp.zeros((GROUPS, local_units * ffn_count), jnp.float32),
        local_bias,
        ffn_place * local_units,
        1,
    )
    grad_w_in, grad_w_out = (
        lax.psum_scatter(
            grad_w_in.astype(jnp.bfloat16), "dp", scatter_dimension=1, tiled=True
        ).astype(jnp.float32),
        lax.psum_scatter(
            grad_w_out.astype(jnp.bfloat16), "dp", scatter_dimension=2, tiled=True
        ).astype(jnp.float32),
    )
    grad_first = grad_second + grad_first_branch
    grad_resid, grad_gain_first, grad_shift_first = normalize_back(
        grad_first, normed_first, inverse_first, gain_rows[0]
    )
    grad_attn = grad_resid.astype(jnp.bfloat16)
    grad_out_bias = jnp.sum(grad_attn, axis=0, dtype=jnp.float32)
    grad_out_full = jnp.einsum("nd,ne->de", context, grad_attn, preferred_element_type=jnp.float32)
    grad_context = jnp.einsum(
        "ne,de->nd", grad_attn, out_all, preferred_element_type=jnp.float32
    ).astype(jnp.bfloat16)

    def attend_back(packed):
        query_slot, key_slot, value_slot, grad_slot, log_slot, length = packed
        logits = slot_scores(query_slot, key_slot, length)
        probabilities = jnp.exp(logits - log_slot[..., None])
        grad_probs = jnp.einsum(
            "qhd,khd->hqk", grad_slot, value_slot, preferred_element_type=jnp.float32
        )
        centre = jnp.sum(probabilities * grad_probs, axis=-1, keepdims=True)
        grad_logits = (probabilities * (grad_probs - centre)).astype(jnp.bfloat16)
        grad_query_slot = (
            jnp.einsum("hqk,khd->qhd", grad_logits, key_slot, preferred_element_type=jnp.float32)
            * score_scale
        )
        grad_key_slot = (
            jnp.einsum("hqk,qhd->khd", grad_logits, query_slot, preferred_element_type=jnp.float32)
            * score_scale
        )
        grad_value_slot = jnp.einsum(
            "hqk,qhd->khd",
            probabilities.astype(jnp.bfloat16),
            grad_slot,
            preferred_element_type=jnp.float32,
        )
        return (
            grad_query_slot.reshape(slot_rows, model_width).astype(jnp.bfloat16),
            grad_key_slot.reshape(slot_rows, model_width).astype(jnp.bfloat16),
            grad_value_slot.reshape(slot_rows, model_width).astype(jnp.bfloat16),
        )

    grad_query, grad_keys, grad_values = lax.map(
        attend_back,
        (
            split_heads(query),
            split_heads(keys),
            split_heads(values),
            split_heads(grad_context),
            log_totals,
            lengths,
        ),
    )
    grad_query = grad_query.reshape(row_count, model_width)
    grad_keys = grad_keys.reshape(row_count, model_width)
    grad_values = grad_values.reshape(row_count, model_width)
    grad_qkv_full = jnp.stack(
        [
            grouped_weight(tokens, grad_query, GROUPS),
            grouped_weight(tokens, grad_keys, GROUPS),
            grouped_weight(tokens, grad_values, GROUPS),
        ]
    ).reshape(3 * model_width, group_width)
    grad_inputs = (
        grad_resid
        + grouped_back(grad_query, projections[0])
        + grouped_back(grad_keys, projections[1])
        + grouped_back(grad_values, projections[2])
    )
    grad_bias_rows = jnp.concatenate(
        [
            grad_inner_bias,
            jnp.stack(
                [
                    jnp.sum(grad_query, axis=0, dtype=jnp.float32),
                    jnp.sum(grad_values, axis=0, dtype=jnp.float32),
                    grad_out_bias,
                    grad_shift_first,
                    grad_out_bias_ffn,
                    grad_shift_second,
                ]
            ),
        ],
        axis=0,
    )
    grad_gain_rows = jnp.stack([grad_gain_first, grad_gain_second])
    grad_qkv_part, grad_out_part, grad_bias_part, grad_gain_part = (
        lax.psum_scatter(grad_qkv_full, ("dp", "ffn"), scatter_dimension=0, tiled=True),
        lax.psum_scatter(grad_out_full, ("dp", "ffn"), scatter_dimension=0, tiled=True),
        lax.psum_scatter(grad_bias_rows, ("dp", "ffn"), scatter_dimension=1, tiled=True),
        lax.psum_scatter(grad_gain_rows, ("dp", "ffn"), scatter_dimension=1, tiled=True),
    )
    return (
        second_norm.astype(jnp.bfloat16),
        grad_inputs.astype(jnp.bfloat16),
        grad_qkv_part,
        grad_out_part,
        grad_w_in,
        grad_w_out,
        grad_bias_part,
        grad_gain_part,
    )


def solution(mesh):
    return jax.shard_map(
        on_device,
        mesh=mesh,
        in_specs=(
            P(("dp", "ffn"), None),
            P(("dp", "ffn")),
            P(("dp", "ffn"), None),
            P(("dp", "ffn"), None),
            P(None, "dp", "ffn"),
            P(None, "ffn", "dp"),
            P(None, ("dp", "ffn")),
            P(None, ("dp", "ffn")),
            P(("dp", "ffn"), None),
        ),
        out_specs=(
            P(("dp", "ffn"), None),
            P(("dp", "ffn"), None),
            P(("dp", "ffn"), None),
            P(("dp", "ffn"), None),
            P(None, "dp", "ffn"),
            P(None, "ffn", "dp"),
            P(None, ("dp", "ffn")),
            P(None, ("dp", "ffn")),
        ),
        check_vma=False,
    )
```

profile of v0, /device:TPU:0, one launch (start us, length us, event | category | flops | bytes accessed | tf_op | source)
XLA Modules:
  0.0 1412.0 jit_solution(7872200745865388336)
XLA Ops:
  8.0 69.5 %all-gather.1 = bf16[32,24,2]{1,2,0:T(2,128)(2,1)S(1)} all-gather(bf16[1,24,2]{1,2,0:T(2,128)(2,1)} %bitcast.263), channel_id=1, replica_groups=mesh['dp'=8,'ffn'=4] {'dp','ffn'}, dimensions={0}, use_global_device_ids=true | all-gather | bytes 3168 | tf_op jit(solution)/shard_map/all_gather | solution.py:74
  77.7 64.6 %all-gather = bf16[32,24,10]{1,2,0:T(8,128)(2,1)S(1)} all-gather(bf16[1,24,10]{1,2,0:T(8,128)(2,1)} %bitcast.262), channel_id=1, replica_groups=mesh['dp'=8,'ffn'=4] {'dp','ffn'}, dimensions={0}, use_global_device_ids=true | all-gather | bytes 15840 | tf_op jit(solution)/shard_map/all_gather | solution.py:73
  143.5 75.9 %all_gather.24 = bf16[2304,192]{1,0:T(8,128)(2,1)S(1)} all-gather(bf16[72,192]{1,0:T(8,128)(2,1)} %param.15), channel_id=1, replica_groups=mesh['dp'=8,'ffn'=4] {'dp','ffn'}, dimensions={0}, use_global_device_ids=true | all-gather | bytes 912384 | tf_op jit(solution)/shard_map/all_gather | solution.py:71
  219.5 3.2 copy.119
  225.1 6.5 convert_element_type.190
  237.3 8.5 reshape.237
  245.8 4.2 add_convert_fusion
  255.1 8.5 reshape.236
  263.6 4.2 add_convert_fusion.1
  269.8 47.1 %while.28 = (s32[]{:T(128)}, bf16[3,512,768]{2,1,0:T(8,128)(2,1)}, f32[3,12,512]{2,1,0:T(8,128)S(1)}, bf16[3,512,12,64]{1,3,2,0:T(8,128)(2,1)}, s32[3]{0:T(128)S...) while((s32[]{:T(128)}, bf16[3,512,768]{2,1,0:T(8,128)(2,1)}, ...), condition=%wide.region_3.4_spmd.clone, body=%wide.region_0.3_spmd.clone.sunk | while | flops 843442688 | bytes 44264568 | solution.py:110
  271.2 4.0 fusion.131
  277.9 5.3 fusion.133
  286.8 4.0 fusion.131
  293.5 5.3 fusion.133
  302.4 4.0 fusion.131
  309.0 5.3 fusion.133
  317.0 5.2 fusion.76
  327.3 9.4 all_gather.29
  336.7 9.2 all_gather.30
  346.0 144.3 %all-gather.8.cloned.1.call-done = bf16[6144,768]{0,1:T(8,128)(2,1)} async-done(((bf16[1536,768]{0,1:T(8,128)(2,1)}), bf16[6144,768]{0,1:T(8,128)(2,1)}) %all-gather.8.cloned.1.call-update) | async-done | bytes 9437200 | tf_op jit(solution)/shard_map/all_gather | solution.py:129
  490.3 12.3 fusion.58
  502.6 5.5 convolution_convert_fusion.1
  509.2 4.7 copy.135
  513.8 154.9 %reduce-scatter.13.cloned.1.call-done = bf16[1536,768]{0,1:T(8,128)(2,1)} async-done(((bf16[6144,768]{0,1:T(8,128)(2,1)}), bf16[1536,768]{0,1:T(8,128)(2,1)}) %reduce-scatter.13.cloned.1.call-update) | async-done | bytes 2359312 | tf_op jit(solution)/shard_map/reduce_scatter | solution.py:133
  668.8 3.9 fusion.74
  679.1 3.6 convert_reduce_fusion.2
  682.7 167.7 %all-gather.10.cloned.1.call-done = bf16[6144,768]{0,1:T(8,128)(2,1)} async-done(((bf16[1536,768]{0,1:T(8,128)(2,1)}), bf16[6144,768]{0,1:T(8,128)(2,1)}) %all-gather.10.cloned.1.call-update) | async-done | bytes 9437200 | tf_op jit(solution)/shard_map/all_gather | solution.py:145
  850.4 14.9 %convert_reduce_fusion = (f32[4,192]{1,0:T(4,128)}, bf16[6144,4,192]{0,2,1:T(8,128)(2,1)S(1)}) fusion(f32[4,6144,192]{1,2,0:T(8,128)} %get-tuple-element.325, f32[4,192]{1,0:T(4,128)S(1)} %constant_dynamic-slice_fusion.2, bf16[6144,4,192]{0,2,1:T(8,128)(2,1)} %bitcast.264, bf16[4,192,192]{1,2,0:T(8,128)(2,1)S(1)} %all_gather.30), kind=kOutput, calls=%fused_computation.73 | convolution fusion | flops 1873280256 | bytes 38049792 | tf_op jit(solution)/shard_map/ngo,gio->ngi/dot_general | solution.py:25
  865.3 5.6 convolution_convert_fusion
  871.9 9.9 convolution_convert_fusion.5
  883.4 9.1 convolution_convert_fusion.4
  893.9 137.5 %reduce-scatter.15.cloned.1.call-done = bf16[1536,768]{0,1:T(8,128)(2,1)} async-done(((bf16[6144,768]{0,1:T(8,128)(2,1)}), bf16[1536,768]{0,1:T(8,128)(2,1)}) %reduce-scatter.15.cloned.1.call-update) | async-done | bytes 2359312 | tf_op jit(solution)/shard_map/reduce_scatter | solution.py:149
  1031.4 9.2 multiply_reduce_fusion.1
  1040.6 4.5 convert_reduce_fusion.3
  1047.2 3.5 convolution_convert_fusion.2
  1050.7 8.2 reshape.252
  1058.9 7.4 copy.139
  1066.3 88.5 %while.29 = (s32[]{:T(128)}, bf16[3,512,768]{1,2,0:T(8,128)(2,1)}, bf16[3,512,768]{1,2,0:T(8,128)(2,1)}, bf16[3,512,768]{1,2,0:T(8,128)(2,1)}, bf16[3,512,12,64]...) while((s32[]{:T(128)}, bf16[3,512,768]{1,2,0:T(8,128)(2,1)}, ...), condition=%wide.region_16.17_spmd.clone, body=%wide.region_14.16_spmd.clone.sunk | while | flops 2062412288 | bytes 116584608 | solution.py:207
  1067.8 3.1 fusion.142
  1074.0 8.3 multiply_reduce_fusion.7
  1082.3 7.1 multiply_convert_fusion.6
  1089.4 3.1 multiply_convert_fusion.8
  1097.1 3.1 fusion.142
  1100.3 3.1 fusion.143
  1103.4 8.3 multiply_reduce_fusion.7
  1111.7 7.1 multiply_convert_fusion.6
  1118.8 3.1 multiply_convert_fusion.8
  1126.6 3.1 fusion.142
  1129.7 3.1 fusion.143
  1132.8 8.3 multiply_reduce_fusion.7
  1141.1 7.1 multiply_convert_fusion.6
  1148.2 3.1 multiply_convert_fusion.8
  1154.8 5.5 copy.175
  1160.3 7.7 reshape.261
  1170.6 3.7 copy.177
  1174.3 7.4 reshape.263
  1181.7 3.5 convolution_bitcast_fusion.2
  1185.2 3.7 copy.176
  1188.9 7.3 reshape.262
  1206.6 6.6 fusion.70
  1225.1 7.6 fusion.66
  1235.2 42.0 %all-reduce.2 = (f32[10,768]{1,0:T(8,128)S(1)}, f32[2,768]{1,0:T(2,128)S(1)}) all-reduce(f32[10,768]{1,0:T(8,128)S(1)} %concatenate.3, f32[2,768]{1,0:T(2,128)S(1)} %pad_maximum_fusion.1), channel_id=8, replica_groups=mesh['dp'=8,'ffn'=4] {'dp','ffn'}, use_global_device_ids=true, to_apply=%region_28.29.clone | all-reduce | flops 9216 | bytes 73728
  1278.5 21.9 %reduce-scatter.17.cloned.1.call-done = f32[72,192]{1,0:T(8,128)} async-done(((f32[2304,192]{1,0:T(8,128)}), f32[72,192]{1,0:T(8,128)}) %reduce-scatter.17.cloned.1.call-update) | async-done | bytes 55312 | tf_op jit(solution)/shard_map/reduce_scatter | solution.py:252
  1300.4 104.8 %reduce-scatter.19.cloned.1.call-done = f32[24,768]{1,0:T(8,128)} async-done(((f32[768,768]{1,0:T(8,128)}), f32[24,768]{1,0:T(8,128)}) %reduce-scatter.19.cloned.1.call-update) | async-done | bytes 73744 | tf_op jit(solution)/shard_map/reduce_scatter | solution.py:253
  (215 shorter events, 100.1 us)
Async XLA Ops:
  7.2 309.8 %all-gather.6.cloned.1.call-start = ((), (), s32[]{:S(2)}) async-start(), calls=%async_computation.6 | async-start | bytes 1216512 | tf_op jit(solution)/shard_map/all_gather | solution.py:72
  7.9 482.4 %all-gather.8.cloned.1.call-start = ((), (), s32[]{:S(2)}) async-start(), calls=%async_computation.7 | async-start | bytes 11796480 | tf_op jit(solution)/shard_map/all_gather | solution.py:129
  142.7 0.7 copy-start.25
  219.5 5.6 copy-start.20
  219.5 14.7 %copy-start.16 = (bf16[768,192]{1,0:T(8,128)(2,1)}, bf16[768,192]{1,0:T(8,128)(2,1)S(1)}, u32[]{:S(2)}) copy-start(bf16[768,192]{1,0:T(8,128)(2,1)S(1)} %get-tuple-element.320) | copy-start | bytes 884740
  219.5 32.5 %copy-start.18 = (bf16[768,192]{1,0:T(8,128)(2,1)}, bf16[768,192]{1,0:T(8,128)(2,1)S(1)}, u32[]{:S(2)}) copy-start(bf16[768,192]{1,0:T(8,128)(2,1)S(1)} %get-tuple-element.321) | copy-start | bytes 884740
  222.8 2.3 copy-start.2
  231.6 2.7 copy-start.3
  250.0 2.1 copy-start.4
  267.7 2.1 copy-start.24
  267.7 2.1 copy-start.42
  269.8 47.1 %copy-start.39 = (f32[768]{0:T(1024)S(1)}, f32[768]{0:T(1024)}, u32[]{:S(2)}) copy-start(f32[768]{0:T(1024)} %get-tuple-element.264) | copy-start | bytes 9220
  322.2 2.1 copy-start
  322.2 2.1 copy-start.26
  322.2 2.1 copy-start.30
  324.3 3.0 copy-start.28
  324.3 12.4 copy-start.29
  326.5 342.3 %reduce-scatter.13.cloned.1.call-start = ((), (), s32[]{:S(2)}) async-start(), calls=%async_computation.8 | async-start | bytes 11796480 | tf_op jit(solution)/shard_map/reduce_scatter | solution.py:133
  502.6 6.5 copy-start.7
  509.1 159.6 %copy-start.32 = (f32[768]{0:T(1024)S(1)}, f32[768]{0:T(1024)}, u32[]{:S(2)}) copy-start(f32[768]{0:T(1024)} %get-tuple-element.262) | copy-start | bytes 9220
  509.1 341.3 %all-gather.10.cloned.1.call-start = ((), (), s32[]{:S(2)}) async-start(), calls=%async_computation.9 | async-start | bytes 11796480 | tf_op jit(solution)/shard_map/all_gather | solution.py:145
  672.6 6.4 copy-start.1
  672.6 3.4 copy-start.6
  672.7 3.4 copy-start.27
  682.7 348.8 %reduce-scatter.15.cloned.1.call-start = ((), (), s32[]{:S(2)}) async-start(), calls=%async_computation.10 | async-start | bytes 11796480 | tf_op jit(solution)/shard_map/reduce_scatter | solution.py:149
  865.3 6.4 copy-start.14
  871.8 329.2 %reduce-scatter.21.cloned.1.call-start = ((), (), s32[]{:S(2)}) async-start(), calls=%async_computation.13 | async-start | bytes 331776
  883.1 148.3 %copy-start.31 = (f32[768]{0:T(1024)S(1)}, f32[768]{0:T(1024)}, u32[]{:S(2)}) copy-start(f32[768]{0:T(1024)} %get-tuple-element.261) | copy-start | bytes 9220
  883.1 318.8 %reduce-scatter.23.cloned.1.call-start = ((), (), s32[]{:S(2)}) async-start(), calls=%async_computation.14 | async-start | bytes 331776
  893.9 406.6 %reduce-scatter.17.cloned.1.call-start = ((), (), s32[]{:S(2)}) async-start(), calls=%async_computation.11 | async-start | bytes 2433024 | tf_op jit(solution)/shard_map/reduce_scatter | solution.py:252
  1040.6 6.6 copy-start.41
  1045.1 2.1 copy-start.8
  1067.8 3.1 copy-start.9
  1097.1 3.1 copy-start.9
  1126.5 3.1 copy-start.9
  1154.8 13.2 copy-start.5
  1168.0 2.6 copy-start.15
  1181.7 3.5 copy-start.22
  1196.2 2.5 copy-start.23
  1198.7 1.8 copy-start.34
  1198.7 1.8 copy-start.33
  1198.7 1.8 copy-start.35
  1198.8 1.8 copy-start.40
  1198.8 5.4 copy-start.37
  1198.8 5.3 copy-start.36
  1198.8 5.4 copy-start.38
  1198.8 5.4 copy-start.13
  1200.4 204.8 %reduce-scatter.19.cloned.1.call-start = ((), (), s32[]{:S(2)}) async-start(), calls=%async_computation.12 | async-start | bytes 2433024 | tf_op jit(solution)/shard_map/reduce_scatter | solution.py:253
  1213.2 4.4 copy-start.12
  1213.2 4.4 copy-start.21
  1217.6 1.7 copy-start.11
  1217.6 1.7 copy-start.19
  1219.3 2.9 copy-start.10
  1219.3 2.9 copy-start.17
Sparse Core Ops, SparseCore 0:
  10.8 56.8 all-gather.5
  326.6 163.6 all-gather.7
  509.2 159.4 reduce-scatter.12
  682.8 167.5 all-gather.9
  871.9 159.4 reduce-scatter.14
  1034.3 33.7 reduce-scatter.20
  1071.2 32.8 reduce-scatter.22
  1200.6 99.8 reduce-scatter.16
  1307.2 98.0 reduce-scatter.18
where the time goes:
time: 1420 us; the launch traced here: 1410 us
  waiting for transfers between devices  732 us (52%)
  blocking collectives  271 us (19%)
  matrix products  181 us (13%)
  local copies, waits for them, and re-layouts  129 us (9%)
  other arithmetic  83.5 us (6%)
  between operations  14.7 us (1%)
    all_gather x1, waiting for transfers between devices, on_device(): grad_gathered = lax.all_gather(grad_branch, 'ffn', axis=0, tiled=True)  168 us
    reduce_scatter x1, waiting for transfers between devices, on_device(): lax.psum_scatter(grouped(act_low, w_out).astype(jnp.bfloat16), 'ffn', sca...  155 us
    all_gather x1, waiting for transfers between devices, on_device(): gathered = lax.all_gather(first_low, 'ffn', axis=0, tiled=True)  144 us
    reduce_scatter x1, waiting for transfers between devices, on_device(): lax.psum_scatter(grouped_back(grad_pre, w_in).astype(jnp.bfloat16), 'ffn'...  137 us
    reduce_scatter x1, waiting for transfers between devices, on_device(): lax.psum_scatter(grad_out_full, ('dp', 'ffn'), scatter_dimension=0, tiled...  105 us
    all_gather x1, blocking collectives, on_device(): lax.all_gather(qkv_weight, ('dp', 'ffn'), axis=0, tiled=True)  75.9 us
    all_gather x1, blocking collectives, on_device(): lax.all_gather(gains, ('dp', 'ffn'), axis=1, tiled=True)  69.5 us
    all_gather x1, blocking collectives, on_device(): lax.all_gather(biases, ('dp', 'ffn'), axis=1, tiled=True)  64.6 us
  transfers between devices with their start and end apart: 9, of which 6 were waited for; matrix products, arithmetic and copies ran while one was open for 23% of the time, Pallas kernels for 0%

commit v1 on v0

v1 whole, which is shorter than its diff:
```python
import functools

import jax
import jax.numpy as jnp
from jax import lax
from jax.experimental import pallas as pl
from jax.experimental.pallas import tpu as pltpu
from jax.sharding import PartitionSpec

f32, bf = jnp.float32, jnp.bfloat16
EPS, NEG = 1e-12, -1e30
SL, D, HEADS, GROUPS, GW, GU = 512, 768, 12, 4, 192, 768
PAIRS = D // 128
R = 256
MESH = pl.DeviceIdType.MESH


def dg(a, b, ca, cb):
    return lax.dot_general(a, b, (((ca,), (cb,)), ((), ())), preferred_element_type=f32)


def nn(a, b):
    return dg(a, b, 1, 0)


def nt(a, b):
    return dg(a, b, 1, 1)


def tn(a, b):
    return dg(a, b, 0, 0)


def win(g):
    return 128 * ((GW * g) // 128)


def off(g):
    return 64 * (g % 2)


def halves(t):
    lane = lax.broadcasted_iota(jnp.int32, t.shape, 1)
    z = jnp.zeros_like(t)
    return jnp.where(lane < 64, t, z), jnp.where(lane < 64, z, t)


def colsum(x):
    return jnp.sum(x, axis=0, keepdims=True)


def rowsum(x):
    return jnp.sum(x, axis=1, keepdims=True)


def gelu_pair(u):
    c = 0.5 + 0.5 * lax.erf(u * 0.7071067811865476)
    return u * c, c + (0.3989422804014327 * u) * jnp.exp((-0.5) * (u * u))


def ln_fwd(r):
    c = r - rowsum(r) * (1.0 / D)
    inv = lax.rsqrt(rowsum(c * c) * (1.0 / D) + EPS)
    return c * inv, inv


def ln_bwd(gy, xh, inv, gamma):
    e = gy * gamma
    return inv * (e - rowsum(e) * (1.0 / D) - xh * (rowsum(e * xh) * (1.0 / D)))


def rows_of(i, size):
    return pl.ds(pl.multiple_of(i * size, size), size)


def project(tok, wq, bias, Q, K, V, s):
    rows = rows_of(s, SL)
    for S in range(2):
        b = 384 * S
        y0, y1 = nn(tok[rows, b:b + 256], wq[2 * S]), nn(tok[rows, b + 128:b + 384], wq[2 * S + 1])
        for part, (dst, brow) in enumerate(((Q, 4), (K, None), (V, 5))):
            c = 256 * part
            tiles = (y0[:, c:c + 128], y0[:, c + 128:c + 256] + y1[:, c:c + 128], y1[:, c + 128:c + 256])
            for i, t in enumerate(tiles):
                cols = slice(b + 128 * i, b + 128 * i + 128)
                if brow is not None:
                    t = t + bias[brow:brow + 1, cols]
                t = t.astype(bf)
                if part == 0:
                    t = t * jnp.asarray(0.125, bf)
                dst[rows, cols] = t


def attend(Q, K, V, P, CTX, LI, maskrow, s, p, T=256):
    r0 = pl.multiple_of(s * SL, SL)
    rows, cols = pl.ds(r0, SL), rows_of(p, 128)
    k = K[rows, cols]
    vcat = jnp.concatenate([jnp.concatenate([a, b], 1) for a, b in
                            zip(halves(V[rows, cols]), halves(jnp.ones((SL, 128), bf)))], 0)
    for t in range(SL // T):
        rt = pl.ds(r0 + t * T, T)
        pbs = []
        for h, q in enumerate(halves(Q[rt, cols])):
            sc = nt(q, k) + maskrow
            pb = jnp.exp(sc - jnp.max(sc, axis=1, keepdims=True)).astype(bf)
            P[h, t * T:(t + 1) * T] = pb
            pbs.append(pb)
        r = nn(jnp.concatenate(pbs, 1), vcat)
        li = 1.0 / r[:, 128:]
        CTX[rt, cols] = r[:, :128] * li
        LI[rt, cols] = li.astype(bf)


def attend_back(Q, K, V, P, CTX, DC, s, p, T=256):
    r0 = pl.multiple_of(s * SL, SL)
    rows, cols = pl.ds(r0, SL), rows_of(p, 128)
    q, k, v, dc = Q[rows, cols], K[rows, cols], V[rows, cols], DC[rows, cols]
    kcat = jnp.concatenate(halves(k), 0)
    dss = [[], []]
    for t in range(SL // T):
        rt = pl.ds(r0 + t * T, T)
        dct = dc[t * T:(t + 1) * T]
        dcs, prods = halves(dct), halves(dct.astype(f32) * CTX[rt, cols])
        row = []
        for h in range(2):
            dp = nt(dcs[h], v) - rowsum(prods[h])
            ds = (P[h, t * T:(t + 1) * T].astype(f32) * dp).astype(bf)
            dss[h].append(ds)
            row.append(ds)
        Q[rt, cols] = (nn(jnp.concatenate(row, 1), kcat) * 0.125).astype(bf)
    dk, dv = [], []
    for h in range(2):
        dk.append(tn(q, jnp.concatenate(dss[h], 0))[64 * h:64 * h + 64])
        dv.append(tn(dc, P[h])[64 * h:64 * h + 64])
    K[rows, cols] = jnp.concatenate(dk, 0).T.astype(bf)
    V[rows, cols] = jnp.concatenate(dv, 0).T.astype(bf)


def middle(i, tok, WO, WI, WT, bias, CTX, DC, DR, OB, G1, G2, G3, GB, AB, SLP, XH, H1B, F):
    rows = rows_of(i, R)
    ctxb = CTX[rows, :].astype(bf)
    xh1, inv1 = ln_fwd(nn(ctxb, WO[...]) + bias[6:7, :] + tok[rows, :].astype(f32))
    XH[...] = xh1
    h1 = xh1 * bias[10:11, :] + bias[7:8, :]
    H1B[...] = h1.astype(bf)
    F[...] = h1 + bias[8:9, :]
    for g in range(GROUPS):
        w = slice(win(g), win(g) + 256)
        a, slope = gelu_pair(nn(H1B[:, w], WI[g]) + bias[g:g + 1, :])
        ab = a.astype(bf)
        AB[g] = ab
        SLP[g] = slope.astype(bf)
        F[:, w] += nt(ab, WT[g])
    xh2, inv2 = ln_fwd(F[...])
    OB[...] = (xh2 * bias[11:12, :] + bias[9:10, :]).astype(bf)
    gy = DC[rows, :].astype(f32)
    GB[11:12, :] += colsum(gy * xh2)
    GB[9:10, :] += colsum(gy)
    dr2 = ln_bwd(gy, xh2, inv2, bias[11:12, :])
    dfb = dr2.astype(bf)
    GB[8:9, :] += colsum(dfb.astype(f32))
    F[...] = dr2
    for g in range(GROUPS):
        w = slice(win(g), win(g) + 256)
        o = off(g)
        dub = (nn(dfb[:, w], WT[g]) * SLP[g].astype(f32)).astype(bf)
        F[:, w] += nt(dub, WI[g])
        GB[g:g + 1, :] += colsum(dub.astype(f32))
        G1[g] += tn(H1B[:, w], dub)[o:o + GW]
        G2[g] += tn(dfb[:, w], AB[g])[o:o + GW]
    xh1, dh1 = XH[...], F[...]
    GB[10:11, :] += colsum(dh1 * xh1)
    GB[7:8, :] += colsum(dh1)
    dab = ln_bwd(dh1, xh1, inv1, bias[10:11, :]).astype(bf)
    GB[6:7, :] += colsum(dab.astype(f32))
    G3[...] += tn(ctxb, dab)
    DC[rows, :] = (nt(dab, WO[...]) * DR[rows, :].astype(f32)).astype(bf)
    DR[rows, :] = dab


def qkv_grads(tok, Q, K, V, G1, GB, s):
    rows = rows_of(s, SL)
    for g in range(GROUPS):
        w = slice(win(g), win(g) + 256)
        d3 = jnp.concatenate([Q[rows, w], K[rows, w], V[rows, w]], axis=1)
        G1[g] += tn(tok[rows, w], d3)[off(g):off(g) + GW]
    GB[4:5, :] += colsum(Q[rows, :].astype(f32))
    GB[5:6, :] += colsum(V[rows, :].astype(f32))


def token_grads(wq, Q, K, V, DR, s):
    rows = rows_of(s, SL)
    for S in range(2):
        b, ys = 384 * S, []
        for g in (2 * S, 2 * S + 1):
            w = slice(win(g), win(g) + 256)
            ys.append(nt(jnp.concatenate([Q[rows, w], K[rows, w], V[rows, w]], axis=1), wq[g]))
        tiles = (ys[0][:, :128], ys[0][:, 128:] + ys[1][:, :128], ys[1][:, 128:])
        for i, t in enumerate(tiles):
            cols = slice(b + 128 * i, b + 128 * i + 128)
            DR[rows, cols] = (t + DR[rows, cols].astype(f32)).astype(bf)


class Cut:
    def __init__(self, nc, nq, nf):
        self.nc, self.nq, self.nf = nc, nq, nf
        self.n = nc * nq * nf
        self.r = D // self.n
        self.a, self.b = GW // (nc * nq), GU // nf
        self.shapes = ((self.r, 640), (self.r, D), (2, self.a, GROUPS * self.b))

    def at(self, d):
        dp, f = divmod(d, self.nf)
        return dp % self.nc, dp // self.nc, f


def unpack_q(cut, GQ, WQ, SM):
    WQ[...] = jnp.zeros_like(WQ)
    r = cut.r
    for p in range(3):
        for g in range(GROUPS):
            parts = []
            for i in range(GW // r):
                d, j = divmod((D * p + GW * g) // r + i, 3)
                parts.append(GQ[cut.at(d)].astype(f32)[:, GW * j:GW * (j + 1)])
            o = off(g)
            WQ[g, o:o + GW, 256 * p + o:256 * p + o + GW] = jnp.concatenate(parts, 0).astype(bf)
    small = jnp.concatenate([GQ[cut.at(d)][:, 512:].astype(f32) for d in range(cut.n)], 0)
    SM[...] = small.T[64:80]


def unpack_o(cut, GO, WO):
    per = GW // cut.r
    for i in range(D // GW):
        rows = [GO[cut.at(d)].astype(f32) for d in range(per * i, per * i + per)]
        WO[GW * i:GW * (i + 1), :] = jnp.concatenate(rows, 0).astype(bf)


def unpack_i(cut, GI, WI, WT):
    b = cut.b
    for k, W in enumerate((WI, WT)):
        for g in range(GROUPS):
            o = off(g)
            z = 0 if o else GW
            W[g, z:z + 64] = jnp.zeros((64, GU), bf)
            cols = []
            for f in range(cut.nf):
                cols.append(jnp.concatenate(
                    [GI[cut.at(dp * cut.nf + f)][k].astype(f32)[:, g * b:(g + 1) * b]
                     for dp in range(cut.nc * cut.nq)], 0))
            W[g, o:o + GW] = jnp.concatenate(cols, 1).astype(bf)


def pack_o(cut, G3, GO):
    for d in range(cut.n):
        GO[cut.at(d)] = G3[cut.r * d:cut.r * (d + 1), :].astype(bf)


def pack_i(cut, G1, G2, GI):
    a, b = cut.a, cut.b
    for k, G in enumerate((G1, G2)):
        for dp in range(cut.nc * cut.nq):
            for f in range(cut.nf):
                GI[cut.at(dp * cut.nf + f) + (k,)] = jnp.concatenate(
                    [G[g, a * dp:a * (dp + 1), b * f:b * (f + 1)] for g in range(GROUPS)], 1).astype(bf)


def pack_q(cut, G1, GB, GQ):
    r = cut.r
    small = jnp.concatenate([jnp.zeros((64, D), f32), GB[...], jnp.zeros((48, D), f32)], 0).T
    for d in range(cut.n):
        parts = []
        for j in range(3):
            p, rest = divmod(r * (3 * d + j), D)
            g, i = divmod(rest, GW)
            c = 256 * p + off(g)
            parts.append(G1[g, i:i + r, c:c + GW])
        parts.append(small[r * d:r * (d + 1), 64:])
        GQ[cut.at(d)] = jnp.concatenate(parts, 1).astype(bf)


class Links:
    def __init__(self, cut, send_sem, recv_sem):
        self.cut, self.sems = cut, (send_sem, recv_sem)
        dp, self.f = lax.axis_index("dp"), lax.axis_index("ffn")
        self.c, self.q = lax.rem(dp, 2), lax.div(dp, 2)
        nq, nf = cut.nq, cut.nf
        self.fs = [lax.rem(self.f + k, nf) for k in range(1, nf)]
        self.qs = [lax.rem(self.q + k, nq) for k in range(1, nq)]
        self.per = nf - 1 + nq - 1 + 1

    def to_f(self, k):
        return (2 * self.q + self.c, self.fs[k])

    def to_q(self, k):
        return (2 * self.qs[k] + self.c, self.f)

    def twin(self):
        return (2 * self.q + 1 - self.c, self.f)

    def greet(self):
        everyone = [self.to_f(k) for k in range(len(self.fs))] + [self.to_q(k) for k in range(len(self.qs))] + [self.twin()]
        barrier = pltpu.get_barrier_semaphore()
        for peer in everyone:
            pl.semaphore_signal(barrier, inc=1, device_id=peer, device_id_type=MESH)
        pl.semaphore_wait(barrier, len(everyone))

    def copy(self, src, dst, slot, peer):
        return pltpu.make_async_remote_copy(
            src_ref=src, dst_ref=dst, send_sem=self.sems[0].at[slot], recv_sem=self.sems[1].at[slot],
            device_id=peer, device_id_type=MESH)

    def gather(self, stage, i, G):
        base = i * self.per
        c, q, f = self.c, self.q, self.f
        if stage == 0:
            return [self.copy(G.at[c, q, f], G.at[c, q, f], base + k, self.to_f(k)) for k in range(len(self.fs))]
        base += len(self.fs)
        if stage == 1:
            return [self.copy(G.at[c, q], G.at[c, q], base + k, self.to_q(k)) for k in range(len(self.qs))]
        return [self.copy(G.at[c], G.at[c], base + len(self.qs), self.twin())]

    def scatter(self, stage, i, G, RC, RP, Z, RF):
        base = (3 + i) * self.per
        c = self.c
        if stage == 0:
            return [self.copy(G.at[1 - c], RC, base, self.twin())]
        base += 1
        if stage == 1:
            return [self.copy(G.at[c, self.qs[k]], RP.at[k], base + k, self.to_q(k)) for k in range(len(self.qs))]
        base += len(self.qs)
        return [self.copy(Z.at[self.fs[k]], RF.at[k], base + k, self.to_f(k)) for k in range(len(self.fs))]

    def add_twin(self, G, RC):
        for q in range(self.cut.nq):
            G[self.c, q] = (G[self.c, q].astype(f32) + RC[q].astype(f32)).astype(bf)

    def add_q(self, G, RP, Z):
        total = G[self.c, self.q].astype(f32)
        for k in range(len(self.qs)):
            total = total + RP[k].astype(f32)
        Z[...] = total.astype(bf)

    def add_f(self, Z, RF):
        total = Z[self.f].astype(f32)
        for k in range(len(self.fs)):
            total = total + RF[k].astype(f32)
        return total


def start(copies):
    for copy in copies:
        copy.start()


def arrive(copies):
    for copy in copies:
        copy.wait_recv()


def sent(copies):
    for copy in copies:
        copy.wait_send()


def layer(cut, remote, length, qp, op, ip, tok_in, cot_in,
          out, gx, phbm, sq, so, si,
          tok, DC, Q, K, V, CTX, DR, WQ, WO, WI, WT, SM, GQ, GO, GI,
          RCq, RCo, RCi, RPq, RPo, RPi, Zq, Zo, Zi, RFq, RFo, RFi,
          G1, G2, G3, GB, AB, SLP, XH, H1B, F, OB, PB, in_sem, p_sem, o_sem, x_sem, *sems):
    slots = tok.shape[0] // SL
    nmid = tok.shape[0] // R
    links = Links(cut, *sems) if remote else None
    loads = [pltpu.make_async_copy(tok_in, tok, in_sem.at[0]), pltpu.make_async_copy(cot_in, DC, in_sem.at[1])]
    start(loads)
    if remote:
        at = links.c, links.q, links.f
        GQ[at] = qp[...]
        GO[at] = op[...]
        GI[at] = ip[...]
    else:
        for src, dst in ((qp, GQ), (op, GO), (ip, GI)):
            pltpu.sync_copy(src, dst)
    gq = lambda stage: links.gather(stage, 0, GQ)
    gr = lambda stage: links.gather(stage, 1, GO) + links.gather(stage, 2, GI)
    sq_args, so_args, si_args = (0, GQ, RCq, RPq, Zq, RFq), (1, GO, RCo, RPo, Zo, RFo), (2, GI, RCi, RPi, Zi, RFi)
    rq = lambda stage: links.scatter(stage, *sq_args)
    rr = lambda stage: links.scatter(stage, *so_args) + links.scatter(stage, *si_args)

    if remote:
        links.greet()
        start(gq(0))
        start(gr(0))
    for G in (G1, G2, G3, GB):
        G[...] = jnp.zeros_like(G)
    if remote:
        arrive(gq(0))
        start(gq(1))
        arrive(gq(1))
        start(gq(2))
        arrive(gr(0))
        start(gr(1))
        arrive(gq(2))
    unpack_q(cut, GQ, WQ, SM)
    loads[0].wait()
    lax.fori_loop(0, slots, lambda s, x: (project(tok, WQ, SM, Q, K, V, s), x)[1], 0)

    steps = slots * PAIRS // 2

    def to_hbm(i, slot):
        return pltpu.make_async_copy(PB.at[slot], phbm.at[i], p_sem.at[slot])

    def forward(i, x):
        half = lax.rem(i, 2)

        @pl.when(i >= 2)
        def _():
            for u in range(2):
                to_hbm(2 * i + u, 2 * half + u).wait()

        if remote:
            @pl.when(i == 4)
            def _():
                arrive(gr(1))
                start(gr(2))

        for u in range(2):
            pair = 2 * i + u
            s = lax.div(pair, PAIRS)
            lane = lax.broadcasted_iota(jnp.int32, (1, SL), 1)
            maskrow = jnp.where(lane < length[s], 0.0, NEG)
            attend(Q, K, V, PB.at[2 * half + u], CTX, DR, maskrow, s, lax.rem(pair, PAIRS))
        for u in range(2):
            to_hbm(2 * i + u, 2 * half + u).start()
        return x

    lax.fori_loop(0, steps, forward, 0)
    if remote:
        arrive(gr(2))
    unpack_o(cut, GO, WO)
    unpack_i(cut, GI, WI, WT)
    loads[1].wait()
    for i in range(max(0, steps - 2), steps):
        for u in range(2):
            to_hbm(2 * i + u, 2 * (i % 2) + u).wait()

    def from_hbm(i, slot):
        return pltpu.make_async_copy(phbm.at[i], PB.at[slot], p_sem.at[slot])

    for u in range(2):
        from_hbm(u, u).start()

    def out_copy(i, slot):
        return pltpu.make_async_copy(OB.at[slot], out.at[rows_of(i, R), :], o_sem.at[slot])

    def mid(i, x):
        slot = lax.rem(i, 2)

        @pl.when(i >= 2)
        def _():
            out_copy(i, slot).wait()

        middle(i, tok, WO, WI, WT, SM, CTX, DC, DR, OB.at[slot], G1, G2, G3, GB, AB, SLP, XH, H1B, F)
        out_copy(i, slot).start()
        return x

    lax.fori_loop(0, nmid, mid, 0)
    if remote:
        sent(gq(0) + gq(1) + gq(2) + gr(0) + gr(1) + gr(2))
    pack_o(cut, G3, GO)
    pack_i(cut, G1, G2, GI)
    if remote:
        start(rr(0))
    G1[...] = jnp.zeros_like(G1)

    def backward(i, x):
        half = lax.rem(i, 2)

        @pl.when(i + 1 < steps)
        def _():
            for u in range(2):
                from_hbm(2 * i + 2 + u, 2 - 2 * half + u).start()

        if remote:
            @pl.when(i == 1)
            def _():
                arrive(rr(0))
                links.add_twin(GO, RCo)
                links.add_twin(GI, RCi)
                start(rr(1))

            @pl.when(i == steps - 2)
            def _():
                arrive(rr(1))
                links.add_q(GO, RPo, Zo)
                links.add_q(GI, RPi, Zi)
                start(rr(2))

        for u in range(2):
            from_hbm(2 * i + u, 2 * half + u).wait()
        for u in range(2):
            pair = 2 * i + u
            attend_back(Q, K, V, PB.at[2 * half + u], CTX, DC, lax.div(pair, PAIRS), lax.rem(pair, PAIRS))
        return x

    lax.fori_loop(0, steps, backward, 0)
    lax.fori_loop(0, slots, lambda s, x: (qkv_grads(tok, Q, K, V, G1, GB, s), x)[1], 0)
    pack_q(cut, G1, GB, GQ)
    if remote:
        start(rq(0))

    def gx_copy(s):
        return pltpu.make_async_copy(DR.at[rows_of(s, SL), :], gx.at[rows_of(s, SL), :], x_sem.at[s])

    def last(s, x):
        if remote:
            @pl.when(s == 1)
            def _():
                arrive(rq(0))
                links.add_twin(GQ, RCq)
                start(rq(1))
        token_grads(WQ, Q, K, V, DR, s)
        gx_copy(s).start()
        return x

    lax.fori_loop(0, slots, last, 0)
    if remote:
        arrive(rr(2))
        so[...] = links.add_f(Zo, RFo)
        si[...] = links.add_f(Zi, RFi)
        arrive(rq(1))
        links.add_q(GQ, RPq, Zq)
        start(rq(2))
        arrive(rq(2))
        sq[...] = links.add_f(Zq, RFq)
        sent(rr(0) + rr(1) + rr(2) + rq(0) + rq(1) + rq(2))
    else:
        for src, dst in ((GQ, sq), (GO, so), (GI, si)):
            pltpu.sync_copy(src, dst)
    for i in range(max(0, nmid - 2), nmid):
        out_copy(i, i % 2).wait()
    for s in range(slots):
        gx_copy(s).wait()


def run_layer(cut, remote, lengths, pieces, tokens, cotangent):
    rows = tokens.shape[0]
    slots = rows // SL
    vm, hbm = pl.BlockSpec(memory_space=pltpu.VMEM), pl.BlockSpec(memory_space=pl.ANY)
    sd, vmem, dma = jax.ShapeDtypeStruct, pltpu.VMEM, pltpu.SemaphoreType.DMA
    nq, nf, shapes = cut.nq, cut.nf, cut.shapes
    scratch = [vmem((rows, D), bf)] * 5 + [vmem((rows, D), f32), vmem((rows, D), bf)]
    scratch += [vmem((GROUPS, 256, 768), bf), vmem((D, D), bf), vmem((GROUPS, 256, GU), bf), vmem((GROUPS, 256, GU), bf), vmem((16, D), f32)]
    scratch += [vmem((cut.nc, nq, nf) + s, bf) for s in shapes]
    if remote:
        for lead in ((nq, nf), (nq - 1, nf), (nf,), (nf - 1,)):
            scratch += [vmem(lead + s, bf) for s in shapes]
    else:
        scratch += [vmem((8, 128), bf)] * 12
    scratch += [vmem((GROUPS, GW, GU), f32)] * 2 + [vmem((D, D), f32), vmem((16, D), f32)]
    scratch += [vmem((GROUPS, R, GU), bf)] * 2 + [vmem((R, D), f32), vmem((R, D), bf), vmem((R, D), f32), vmem((2, R, D), bf)]
    scratch += [vmem((4, 2, SL, SL), bf), dma((2,)), dma((4,)), dma((2,)), dma((slots,))]
    params = dict(vmem_limit_bytes=64 * 1024 * 1024 - 65536)
    if remote:
        count = 6 * (nf + nq - 1)
        scratch += [dma((count,)), dma((count,))]
        params.update(collective_id=0, has_side_effects=True)
    return pl.pallas_call(
        functools.partial(layer, cut, remote),
        out_shape=(sd((rows, D), bf), sd((rows, D), bf), sd((slots * PAIRS, 2, SL, SL), bf)) + tuple(sd(s, f32) if remote else sd((cut.nc, nq, nf) + s, bf) for s in shapes),
        in_specs=[pl.BlockSpec(memory_space=pltpu.SMEM)] + [vm if remote else hbm] * 3 + [hbm, hbm],
        out_specs=(hbm, hbm, hbm) + (vm if remote else hbm,) * 3,
        scratch_shapes=scratch,
        compiler_params=pltpu.CompilerParams(**params),
    )(lengths, *pieces, tokens, cotangent)


def on_device(cut, remote, tokens, lengths, qkv_weight, out_weight, ffn_in_weight, ffn_out_weight, biases, gains, cotangent):
    r, a, b = cut.r, cut.a, cut.b
    q_piece = jnp.concatenate(
        [qkv_weight.reshape(3, r, GW).transpose(1, 0, 2).reshape(r, 3 * GW), biases.T, gains.T, jnp.zeros((r, 52), bf)], axis=1)
    i_piece = jnp.stack([ffn_in_weight.transpose(1, 0, 2).reshape(a, GROUPS * b), ffn_out_weight.transpose(2, 0, 1).reshape(a, GROUPS * b)])
    out, gx, _, sq, so, si = run_layer(cut, remote, lengths, (q_piece, out_weight, i_piece), tokens, cotangent)
    g_qkv = sq[:, :3 * GW].reshape(r, 3, GW).transpose(1, 0, 2).reshape(3 * r, GW)
    g_in = si[0].reshape(a, GROUPS, b).transpose(1, 0, 2)
    g_out = si[1].reshape(a, GROUPS, b).transpose(1, 2, 0)
    return out, gx, g_qkv, so, g_in, g_out, sq[:, 576:586].T, sq[:, 586:588].T


def solution(mesh):
    both = ("dp", "ffn")
    P = PartitionSpec
    return jax.shard_map(
        functools.partial(on_device, Cut(2, mesh.shape["dp"] // 2, mesh.shape["ffn"]), True),
        mesh=mesh,
        in_specs=(P(both, None), P(both), P(both, None), P(both, None), P(None, "dp", "ffn"),
                  P(None, "ffn", "dp"), P(None, both), P(None, both), P(both, None)),
        out_specs=(P(both, None), P(both, None), P(both, None), P(both, None), P(None, "dp", "ffn"),
                   P(None, "ffn", "dp"), P(None, both), P(None, both)),
        check_vma=False,
    )
```

time: 1420 us -> 152 us (0.11)
  waiting for transfers between devices: 732 us -> 0 us
  blocking collectives: 271 us -> 0 us
  matrix products: 181 us -> 0 us
  Pallas kernels: 0 us -> 133 us
  local copies, waits for them, and re-layouts: 129 us -> 16.1 us
  other arithmetic: 83.5 us -> 1.33 us
    reduce_scatter x4 -> x0, waiting for transfers between devices: 419 us -> none  [the longest x1 155 us: on_device(): lax.psum_scatter(grouped(act_low, w_out).astype(jnp.bfloat16), 'ffn', sca...]
    all_gather x3 -> x0, waiting for transfers between devices: 312 us -> none  [the longest x1 168 us: on_device(): grad_gathered = lax.all_gather(grad_branch, 'ffn', axis=0, tiled=True)]
    all_gather x5 -> x0, blocking collectives: 229 us -> none  [the longest x1 75.9 us: on_device(): lax.all_gather(qkv_weight, ('dp', 'ffn'), axis=0, tiled=True)]
    dot_general x39 -> x0, matrix products: 181 us -> none  [the longest x5 27.6 us: grouped_weight(): jnp.einsum('ngi,ngo->gio', values.reshape(count, group_count, -1), gradie...]
    pallas_call x0 -> x1, Pallas kernels: none -> 133 us  [run_layer(): pl.pallas_call(functools.partial(layer, cut, remote), out_shape=(sd((rows...]
    unnamed x1 -> x0, blocking collectives: 42 us -> none
    convert_element_type x9 -> x0, other arithmetic: 40.6 us -> none  [the longest x3 21.3 us: attend_back(): grad_logits = (probabilities * (grad_probs - centre)).astype(jnp.bfloat16)]
    reduce_sum x12 -> x0, other arithmetic: 37.3 us -> none  [the longest x2 12.2 us: normalize_back(): jnp.sum(upstream * normed, axis=0)]
  transfers between devices with their start and end apart: 9 -> 0, of which waited for: 6 -> 0; matrix products, arithmetic and copies ran while one was open for 23% -> 0% of each run, Pallas kernels for 0% -> 0%
where the time goes in v1:
time: 152 us; the launch traced here: 151 us
  Pallas kernels  133 us (88%)
  local copies, waits for them, and re-layouts  16.1 us (11%)
    pallas_call x1, Pallas kernels, run_layer(): pl.pallas_call(functools.partial(layer, cut, remote), out_shape=(sd((rows...  133 us
    unnamed x11, local copies, waits for them, and re-layouts  8.25 us

profile of v1, /device:TPU:0, one launch (start us, length us, event | category | flops | bytes accessed | tf_op | source)
XLA Modules:
  0.0 150.9 jit_solution(17130756009778987769)
XLA Ops:
  0.6 0.1 pad.5.clone
  0.7 0.8 copy.37
  1.5 0.7 copy.38
  2.2 0.8 copy.49
  3.0 0.1 reshape.29
  3.1 0.7 maximum_maximum_fusion.qp
  3.8 0.8 copy.39
  4.6 0.1 stack_reshape.6
  4.7 0.8 copy.40
  5.6 0.1 stack_reshape.7
  5.7 0.6 pad_maximum_fusion.ip
  6.3 132.8 %shard_map.152 = (bf16[1536,768]{1,0:T(8,128)(2,1)}, bf16[1536,768]{1,0:T(8,128)(2,1)}, bf16[18,2,512,512]{3,2,1,0:T(8,128)(2,1)}, f32[24,640]{1,0:T(8,128)}, f32[24,768]{1,0:T(8,128)}, /*index=5*/f32[2,24,768]{2,1,0:T(8,128)}) custom-call(s32[3]{0:T(128)} %length.1, bf16[24,640]{1,0:T(8,128)(2,1)} %maximum_maximum_fusion.qp, bf16[24,768]{1,0:T(8,128)(2,1)} %op.1, ...), custom_call_target="tpu_custom_call" | custom-call | tf_op jit(solution)/shard_map/pallas_call | solution.py:568
  139.2 0.8 slice_bitcast_fusion
  140.0 0.6 copy.45
  140.6 0.8 slice_bitcast_fusion.1
  141.4 0.7 copy.44
  142.0 0.9 reshape.30
  143.0 0.6 copy.41
  143.6 0.9 fusion
  144.6 0.1 reshape_squeeze.7
  144.7 0.1 reshape_squeeze.6
  144.8 0.7 copy_bitcast_fusion
  145.5 0.0 copy-start
  145.5 3.4 %copy.53 = bf16[1536,768]{1,0:T(8,128)(2,1)} copy(bf16[1536,768]{1,0:T(8,128)(2,1)} %get-tuple-element.54) | data formatting | bytes 4718592
  148.9 0.0 copy-done
  148.9 0.0 copy-start.1
  148.9 1.4 copy.54
  150.3 0.0 copy-done.1
  150.3 0.6 copy.55
  (1 shorter events, 0.0 us)
Async XLA Ops:
  145.5 3.4 %copy-start = (bf16[1536,768]{1,0:T(8,128)(2,1)S(1)}, bf16[1536,768]{1,0:T(8,128)(2,1)}, u32[]{:S(2)}) copy-start(bf16[1536,768]{1,0:T(8,128)(2,1)} %get-tuple-element.55) | copy-start | bytes 7077892
  148.9 1.4 copy-start.1

commit v2 on v1

--- a/solution.py
+++ b/solution.py
@@ -201,20 +201,41 @@
             DR[rows, cols] = (t + DR[rows, cols].astype(f32)).astype(bf)
 
 
+QA, QB, OW, FW = range(4)
+ORDER = ("qf", "fq", "fq", "qf")
+
+
 class Cut:
-    def __init__(self, nc, nq, nf):
-        self.nc, self.nq, self.nf = nc, nq, nf
-        self.n = nc * nq * nf
+    def __init__(self, nq, nf):
+        self.nq, self.nf = nq, nf
+        self.n = 2 * nq * nf
         self.r = D // self.n
-        self.a, self.b = GW // (nc * nq), GU // nf
-        self.shapes = ((self.r, 640), (self.r, D), (2, self.a, GROUPS * self.b))
-
-    def at(self, d):
+        self.a, self.b = GW // (2 * nq), GU // nf
+        self.shapes = ((self.r, 2 * GW), (self.r, 256), (self.r, D), (2, self.a, GROUPS * self.b))
+
+    def lead(self, i):
+        return (self.nq, self.nf) if ORDER[i] == "qf" else (self.nf, self.nq)
+
+    def at(self, i, d):
         dp, f = divmod(d, self.nf)
-        return dp % self.nc, dp // self.nc, f
-
-
-def unpack_q(cut, GQ, WQ, SM):
+        c, q = dp % 2, dp // 2
+        return (c, q, f) if ORDER[i] == "qf" else (c, f, q)
+
+
+def put_pieces(cut, at, qkv, wo, wi, wt, biases, gains, SC, G):
+    r = cut.r
+    SC[...] = jnp.zeros_like(SC)
+    SC[0:10, 0:r] = biases[...].astype(f32)
+    SC[10:12, 0:r] = gains[...].astype(f32)
+    rows = qkv[...].astype(f32)
+    G[QA][at[QA]] = jnp.concatenate([rows[:r], rows[r:2 * r]], 1).astype(bf)
+    G[QB][at[QB]] = jnp.concatenate([rows[2 * r:], SC[...].T[:r, :64]], 1).astype(bf)
+    G[OW][at[OW]] = wo[...]
+    for k, w in enumerate((wi, wt)):
+        G[FW][at[FW] + (k,)] = jnp.concatenate([w[g].astype(f32) for g in range(GROUPS)], 1).astype(bf)
+
+
+def unpack_q(cut, G, WQ, SM):
     WQ[...] = jnp.zeros_like(WQ)
     r = cut.r
     for p in range(3):
@@ -222,21 +243,24 @@
             parts = []
             for i in range(GW // r):
                 d, j = divmod((D * p + GW * g) // r + i, 3)
-                parts.append(GQ[cut.at(d)].astype(f32)[:, GW * j:GW * (j + 1)])
+                if j < 2:
+                    parts.append(G[QA][cut.at(QA, d)].astype(f32)[:, GW * j:GW * (j + 1)])
+                else:
+                    parts.append(G[QB][cut.at(QB, d)].astype(f32)[:, :GW])
             o = off(g)
             WQ[g, o:o + GW, 256 * p + o:256 * p + o + GW] = jnp.concatenate(parts, 0).astype(bf)
-    small = jnp.concatenate([GQ[cut.at(d)][:, 512:].astype(f32) for d in range(cut.n)], 0)
+    small = jnp.concatenate([G[QB][cut.at(QB, d)][:, 128:].astype(f32) for d in range(cut.n)], 0)
     SM[...] = small.T[64:80]
 
 
-def unpack_o(cut, GO, WO):
+def unpack_o(cut, G, WO):
     per = GW // cut.r
     for i in range(D // GW):
-        rows = [GO[cut.at(d)].astype(f32) for d in range(per * i, per * i + per)]
+        rows = [G[OW][cut.at(OW, d)].astype(f32) for d in range(per * i, per * i + per)]
         WO[GW * i:GW * (i + 1), :] = jnp.concatenate(rows, 0).astype(bf)
 
 
-def unpack_i(cut, GI, WI, WT):
+def unpack_f(cut, G, WI, WT):
     b = cut.b
     for k, W in enumerate((WI, WT)):
         for g in range(GROUPS):
@@ -246,26 +270,25 @@
             cols = []
             for f in range(cut.nf):
                 cols.append(jnp.concatenate(
-                    [GI[cut.at(dp * cut.nf + f)][k].astype(f32)[:, g * b:(g + 1) * b]
-                     for dp in range(cut.nc * cut.nq)], 0))
+                    [G[FW][cut.at(FW, dp * cut.nf + f)][k].astype(f32)[:, g * b:(g + 1) * b] for dp in range(2 * cut.nq)], 0))
             W[g, o:o + GW] = jnp.concatenate(cols, 1).astype(bf)
 
 
-def pack_o(cut, G3, GO):
+def pack_o(cut, G3, G):
     for d in range(cut.n):
-        GO[cut.at(d)] = G3[cut.r * d:cut.r * (d + 1), :].astype(bf)
-
-
-def pack_i(cut, G1, G2, GI):
+        G[OW][cut.at(OW, d)] = G3[cut.r * d:cut.r * (d + 1), :].astype(bf)
+
+
+def pack_f(cut, G1, G2, G):
     a, b = cut.a, cut.b
-    for k, G in enumerate((G1, G2)):
-        for dp in range(cut.nc * cut.nq):
+    for k, grad in enumerate((G1, G2)):
+        for dp in range(2 * cut.nq):
             for f in range(cut.nf):
-                GI[cut.at(dp * cut.nf + f) + (k,)] = jnp.concatenate(
-                    [G[g, a * dp:a * (dp + 1), b * f:b * (f + 1)] for g in range(GROUPS)], 1).astype(bf)
-
-
-def pack_q(cut, G1, GB, GQ):
+                G[FW][cut.at(FW, dp * cut.nf + f) + (k,)] = jnp.concatenate(
+                    [grad[g, a * dp:a * (dp + 1), b * f:b * (f + 1)] for g in range(GROUPS)], 1).astype(bf)
+
+
+def pack_q(cut, G1, GB, G):
     r = cut.r
     small = jnp.concatenate([jnp.zeros((64, D), f32), GB[...], jnp.zeros((48, D), f32)], 0).T
     for d in range(cut.n):
@@ -275,8 +298,8 @@
             g, i = divmod(rest, GW)
             c = 256 * p + off(g)
             parts.append(G1[g, i:i + r, c:c + GW])
-        parts.append(small[r * d:r * (d + 1), 64:])
-        GQ[cut.at(d)] = jnp.concatenate(parts, 1).astype(bf)
+        G[QA][cut.at(QA, d)] = jnp.concatenate(parts[:2], 1).astype(bf)
+        G[QB][cut.at(QB, d)] = jnp.concatenate([parts[2], small[r * d:r * (d + 1), 64:]], 1).astype(bf)
 
 
 class Links:
@@ -285,25 +308,23 @@
         dp, self.f = lax.axis_index("dp"), lax.axis_index("ffn")
         self.c, self.q = lax.rem(dp, 2), lax.div(dp, 2)
         nq, nf = cut.nq, cut.nf
-        self.fs = [lax.rem(self.f + k, nf) for k in range(1, nf)]
-        self.qs = [lax.rem(self.q + k, nq) for k in range(1, nq)]
-        self.per = nf - 1 + nq - 1 + 1
-
-    def to_f(self, k):
-        return (2 * self.q + self.c, self.fs[k])
-
-    def to_q(self, k):
-        return (2 * self.qs[k] + self.c, self.f)
-
-    def twin(self):
-        return (2 * self.q + 1 - self.c, self.f)
+        fs = [lax.rem(self.f + k, nf) for k in range(1, nf)]
+        qs = [lax.rem(self.q + k, nq) for k in range(1, nq)]
+        to_f = [(2 * self.q + self.c, f) for f in fs]
+        to_q = [(2 * q + self.c, self.f) for q in qs]
+        self.twin = (2 * self.q + 1 - self.c, self.f)
+        self.axis = {"q": (self.q, qs, to_q), "f": (self.f, fs, to_f)}
+        self.per = nf + nq - 1
+
+    def at(self, i):
+        return (self.c, self.q, self.f) if ORDER[i] == "qf" else (self.c, self.f, self.q)
 
     def greet(self):
-        everyone = [self.to_f(k) for k in range(len(self.fs))] + [self.to_q(k) for k in range(len(self.qs))] + [self.twin()]
         barrier = pltpu.get_barrier_semaphore()
+        everyone = self.axis["q"][2] + self.axis["f"][2] + [self.twin]
         for peer in everyone:
             pl.semaphore_signal(barrier, inc=1, device_id=peer, device_id_type=MESH)
-        pl.semaphore_wait(barrier, len(everyone))
+        return lambda: pl.semaphore_wait(barrier, len(everyone))
 
     def copy(self, src, dst, slot, peer):
         return pltpu.make_async_remote_copy(
@@ -311,40 +332,40 @@
             device_id=peer, device_id_type=MESH)
 
     def gather(self, stage, i, G):
-        base = i * self.per
-        c, q, f = self.c, self.q, self.f
+        base, c = i * self.per, self.c
+        (u, us, to_u), (v, vs, to_v) = (self.axis[x] for x in ORDER[i])
         if stage == 0:
-            return [self.copy(G.at[c, q, f], G.at[c, q, f], base + k, self.to_f(k)) for k in range(len(self.fs))]
-        base += len(self.fs)
+            return [self.copy(G.at[c, u, v], G.at[c, u, v], base + k, to_v[k]) for k in range(len(vs))]
+        base += len(vs)
         if stage == 1:
-            return [self.copy(G.at[c, q], G.at[c, q], base + k, self.to_q(k)) for k in range(len(self.qs))]
-        return [self.copy(G.at[c], G.at[c], base + len(self.qs), self.twin())]
-
-    def scatter(self, stage, i, G, RC, RP, Z, RF):
-        base = (3 + i) * self.per
-        c = self.c
+            return [self.copy(G.at[c, u], G.at[c, u], base + k, to_u[k]) for k in range(len(us))]
+        return [self.copy(G.at[c], G.at[c], base + len(us), self.twin)]
+
+    def scatter(self, stage, i, G, RC, RU, Z, RV):
+        base, c = (4 + i) * self.per, self.c
+        (u, us, to_u), (v, vs, to_v) = (self.axis[x] for x in ORDER[i])
         if stage == 0:
-            return [self.copy(G.at[1 - c], RC, base, self.twin())]
+            return [self.copy(G.at[1 - c], RC, base, self.twin)]
         base += 1
         if stage == 1:
-            return [self.copy(G.at[c, self.qs[k]], RP.at[k], base + k, self.to_q(k)) for k in range(len(self.qs))]
-        base += len(self.qs)
-        return [self.copy(Z.at[self.fs[k]], RF.at[k], base + k, self.to_f(k)) for k in range(len(self.fs))]
-
-    def add_twin(self, G, RC):
-        for q in range(self.cut.nq):
-            G[self.c, q] = (G[self.c, q].astype(f32) + RC[q].astype(f32)).astype(bf)
-
-    def add_q(self, G, RP, Z):
-        total = G[self.c, self.q].astype(f32)
-        for k in range(len(self.qs)):
-            total = total + RP[k].astype(f32)
+            return [self.copy(G.at[c, us[k]], RU.at[k], base + k, to_u[k]) for k in range(len(us))]
+        base += len(us)
+        return [self.copy(Z.at[vs[k]], RV.at[k], base + k, to_v[k]) for k in range(len(vs))]
+
+    def add_twin(self, i, G, RC, RU, Z, RV):
+        for u in range(G.shape[1]):
+            G[self.c, u] = (G[self.c, u].astype(f32) + RC[u].astype(f32)).astype(bf)
+
+    def add_u(self, i, G, RC, RU, Z, RV):
+        total = G[self.c, self.axis[ORDER[i][0]][0]].astype(f32)
+        for k in range(RU.shape[0]):
+            total = total + RU[k].astype(f32)
         Z[...] = total.astype(bf)
 
-    def add_f(self, Z, RF):
-        total = Z[self.f].astype(f32)
-        for k in range(len(self.fs)):
-            total = total + RF[k].astype(f32)
+    def add_v(self, i, G, RC, RU, Z, RV):
+        total = Z[self.axis[ORDER[i][1]][0]].astype(f32)
+        for k in range(RV.shape[0]):
+            total = total + RV[k].astype(f32)
         return total
 
 
@@ -363,45 +384,52 @@
         copy.wait_send()
 
 
-def layer(cut, remote, length, qp, op, ip, tok_in, cot_in,
-          out, gx, phbm, sq, so, si,
-          tok, DC, Q, K, V, CTX, DR, WQ, WO, WI, WT, SM, GQ, GO, GI,
-          RCq, RCo, RCi, RPq, RPo, RPi, Zq, Zo, Zi, RFq, RFo, RFi,
-          G1, G2, G3, GB, AB, SLP, XH, H1B, F, OB, PB, in_sem, p_sem, o_sem, x_sem, *sems):
+def layer(cut, remote, length, *refs):
+    count = 6 if remote else 4
+    pieces, refs = refs[:count], refs[count:]
+    tok_in, cot_in, out, gx, phbm = refs[:5]
+    results, refs = refs[5:9], refs[9:]
+    tok, DC, Q, K, V, CTX, DR, WQ, WO, WI, WT, SM = refs[:12]
+    G, refs = refs[12:16], refs[16:]
+    if remote:
+        parts, refs = [refs[4 * k:4 * k + 4] for k in range(4)], refs[16:]
+        RC, RU, Z, RV = parts
+    G1, G2, G3, GB, SC, AB, SLP, XH, H1B, F, OB, PB, in_sem, p_sem, o_sem, x_sem = refs[:16]
     slots = tok.shape[0] // SL
     nmid = tok.shape[0] // R
-    links = Links(cut, *sems) if remote else None
+    links = Links(cut, *refs[16:]) if remote else None
+
+    def gather(stage, which):
+        return sum((links.gather(stage, i, G[i]) for i in which), [])
+
+    def scatter(stage, which):
+        return sum((links.scatter(stage, i, G[i], RC[i], RU[i], Z[i], RV[i]) for i in which), [])
+
+    def add(step, which):
+        return [step(i, G[i], RC[i], RU[i], Z[i], RV[i]) for i in which]
+
+    early, late = (QA, QB), (OW, FW)
+    if remote:
+        met = links.greet()
     loads = [pltpu.make_async_copy(tok_in, tok, in_sem.at[0]), pltpu.make_async_copy(cot_in, DC, in_sem.at[1])]
     start(loads)
     if remote:
-        at = links.c, links.q, links.f
-        GQ[at] = qp[...]
-        GO[at] = op[...]
-        GI[at] = ip[...]
+        put_pieces(cut, [links.at(i) for i in range(4)], *pieces, SC, G)
+        met()
+        start(gather(0, early))
     else:
-        for src, dst in ((qp, GQ), (op, GO), (ip, GI)):
+        for src, dst in zip(pieces, G):
             pltpu.sync_copy(src, dst)
-    gq = lambda stage: links.gather(stage, 0, GQ)
-    gr = lambda stage: links.gather(stage, 1, GO) + links.gather(stage, 2, GI)
-    sq_args, so_args, si_args = (0, GQ, RCq, RPq, Zq, RFq), (1, GO, RCo, RPo, Zo, RFo), (2, GI, RCi, RPi, Zi, RFi)
-    rq = lambda stage: links.scatter(stage, *sq_args)
-    rr = lambda stage: links.scatter(stage, *so_args) + links.scatter(stage, *si_args)
-
-    if remote:
-        links.greet()
-        start(gq(0))
-        start(gr(0))
-    for G in (G1, G2, G3, GB):
-        G[...] = jnp.zeros_like(G)
-    if remote:
-        arrive(gq(0))
-        start(gq(1))
-        arrive(gq(1))
-        start(gq(2))
-        arrive(gr(0))
-        start(gr(1))
-        arrive(gq(2))
-    unpack_q(cut, GQ, WQ, SM)
+    for g in (G1, G2, G3, GB):
+        g[...] = jnp.zeros_like(g)
+    if remote:
+        arrive(gather(0, early))
+        start(gather(1, early))
+        arrive(gather(1, early))
+        start(gather(2, early))
+        start(gather(0, late))
+        arrive(gather(2, early))
+    unpack_q(cut, G, WQ, SM)
     loads[0].wait()
     lax.fori_loop(0, slots, lambda s, x: (project(tok, WQ, SM, Q, K, V, s), x)[1], 0)
 
@@ -419,10 +447,10 @@
                 to_hbm(2 * i + u, 2 * half + u).wait()
 
         if remote:
-            @pl.when(i == 4)
+            @pl.when(i == 1)
             def _():
-                arrive(gr(1))
-                start(gr(2))
+                arrive(gather(0, late))
+                start(gather(1, late))
 
         for u in range(2):
             pair = 2 * i + u
@@ -436,9 +464,11 @@
 
     lax.fori_loop(0, steps, forward, 0)
     if remote:
-        arrive(gr(2))
-    unpack_o(cut, GO, WO)
-    unpack_i(cut, GI, WI, WT)
+        arrive(gather(1, late))
+        start(gather(2, late))
+        arrive(gather(2, late))
+    unpack_o(cut, G, WO)
+    unpack_f(cut, G, WI, WT)
     loads[1].wait()
     for i in range(max(0, steps - 2), steps):
         for u in range(2):
@@ -466,11 +496,11 @@
 
     lax.fori_loop(0, nmid, mid, 0)
     if remote:
-        sent(gq(0) + gq(1) + gq(2) + gr(0) + gr(1) + gr(2))
-    pack_o(cut, G3, GO)
-    pack_i(cut, G1, G2, GI)
-    if remote:
-        start(rr(0))
+        sent(sum((gather(stage, early + late) for stage in range(3)), []))
+    pack_o(cut, G3, G)
+    pack_f(cut, G1, G2, G)
+    if remote:
+        start(scatter(0, late))
     G1[...] = jnp.zeros_like(G1)
 
     def backward(i, x):
@@ -484,17 +514,15 @@
         if remote:
             @pl.when(i == 1)
             def _():
-                arrive(rr(0))
-                links.add_twin(GO, RCo)
-                links.add_twin(GI, RCi)
-                start(rr(1))
-
-            @pl.when(i == steps - 2)
+                arrive(scatter(0, late))
+                add(links.add_twin, late)
+                start(scatter(1, late))
+
+            @pl.when(i == steps - 1)
             def _():
-                arrive(rr(1))
-                links.add_q(GO, RPo, Zo)
-                links.add_q(GI, RPi, Zi)
-                start(rr(2))
+                arrive(scatter(1, late))
+                add(links.add_u, late)
+                start(scatter(2, late))
 
         for u in range(2):
             from_hbm(2 * i + u, 2 * half + u).wait()
@@ -505,9 +533,9 @@
 
     lax.fori_loop(0, steps, backward, 0)
     lax.fori_loop(0, slots, lambda s, x: (qkv_grads(tok, Q, K, V, G1, GB, s), x)[1], 0)
-    pack_q(cut, G1, GB, GQ)
-    if remote:
-        start(rq(0))
+    pack_q(cut, G1, GB, G)
+    if remote:
+        start(scatter(0, early))
 
     def gx_copy(s):
         return pltpu.make_async_copy(DR.at[rows_of(s, SL), :], gx.at[rows_of(s, SL), :], x_sem.at[s])
@@ -516,26 +544,27 @@
         if remote:
             @pl.when(s == 1)
             def _():
-                arrive(rq(0))
-                links.add_twin(GQ, RCq)
-                start(rq(1))
+                arrive(scatter(0, early))
+                add(links.add_twin, early)
+                start(scatter(1, early))
         token_grads(WQ, Q, K, V, DR, s)
         gx_copy(s).start()
         return x
 
     lax.fori_loop(0, slots, last, 0)
     if remote:
-        arrive(rr(2))
-        so[...] = links.add_f(Zo, RFo)
-        si[...] = links.add_f(Zi, RFi)
-        arrive(rq(1))
-        links.add_q(GQ, RPq, Zq)
-        start(rq(2))
-        arrive(rq(2))
-        sq[...] = links.add_f(Zq, RFq)
-        sent(rr(0) + rr(1) + rr(2) + rq(0) + rq(1) + rq(2))
+        arrive(scatter(2, late))
+        for i, total in zip(late, add(links.add_v, late)):
+            results[i][...] = total
+        arrive(scatter(1, early))
+        add(links.add_u, early)
+        start(scatter(2, early))
+        arrive(scatter(2, early))
+        for i, total in zip(early, add(links.add_v, early)):
+            results[i][...] = total
+        sent(sum((scatter(stage, early + late) for stage in range(3)), []))
     else:
-        for src, dst in ((GQ, sq), (GO, so), (GI, si)):
+        for src, dst in zip(G, results):
             pltpu.sync_copy(src, dst)
     for i in range(max(0, nmid - 2), nmid):
         out_copy(i, i % 2).wait()
@@ -548,50 +577,86 @@
     slots = rows // SL
     vm, hbm = pl.BlockSpec(memory_space=pltpu.VMEM), pl.BlockSpec(memory_space=pl.ANY)
     sd, vmem, dma = jax.ShapeDtypeStruct, pltpu.VMEM, pltpu.SemaphoreType.DMA
-    nq, nf, shapes = cut.nq, cut.nf, cut.shapes
+    shapes, leads = cut.shapes, [cut.lead(i) for i in range(4)]
     scratch = [vmem((rows, D), bf)] * 5 + [vmem((rows, D), f32), vmem((rows, D), bf)]
     scratch += [vmem((GROUPS, 256, 768), bf), vmem((D, D), bf), vmem((GROUPS, 256, GU), bf), vmem((GROUPS, 256, GU), bf), vmem((16, D), f32)]
-    scratch += [vmem((cut.nc, nq, nf) + s, bf) for s in shapes]
-    if remote:
-        for lead in ((nq, nf), (nq - 1, nf), (nf,), (nf - 1,)):
-            scratch += [vmem(lead + s, bf) for s in shapes]
-    else:
-        scratch += [vmem((8, 128), bf)] * 12
-    scratch += [vmem((GROUPS, GW, GU), f32)] * 2 + [vmem((D, D), f32), vmem((16, D), f32)]
+    scratch += [vmem((2,) + u + s, bf) for u, s in zip(leads, shapes)]
+    if remote:
+        scratch += [vmem(u + s, bf) for u, s in zip(leads, shapes)]
+        scratch += [vmem((u[0] - 1, u[1]) + s, bf) for u, s in zip(leads, shapes)]
+        scratch += [vmem(u[1:] + s, bf) for u, s in zip(leads, shapes)]
+        scratch += [vmem((u[1] - 1,) + s, bf) for u, s in zip(leads, shapes)]
+    scratch += [vmem((GROUPS, GW, GU), f32)] * 2 + [vmem((D, D), f32), vmem((16, D), f32), vmem((128, 128), f32)]
     scratch += [vmem((GROUPS, R, GU), bf)] * 2 + [vmem((R, D), f32), vmem((R, D), bf), vmem((R, D), f32), vmem((2, R, D), bf)]
     scratch += [vmem((4, 2, SL, SL), bf), dma((2,)), dma((4,)), dma((2,)), dma((slots,))]
     params = dict(vmem_limit_bytes=64 * 1024 * 1024 - 65536)
     if remote:
-        count = 6 * (nf + nq - 1)
+        count = 8 * (cut.nf + cut.nq - 1)
         scratch += [dma((count,)), dma((count,))]
         params.update(collective_id=0, has_side_effects=True)
     return pl.pallas_call(
         functools.partial(layer, cut, remote),
-        out_shape=(sd((rows, D), bf), sd((rows, D), bf), sd((slots * PAIRS, 2, SL, SL), bf)) + tuple(sd(s, f32) if remote else sd((cut.nc, nq, nf) + s, bf) for s in shapes),
-        in_specs=[pl.BlockSpec(memory_space=pltpu.SMEM)] + [vm if remote else hbm] * 3 + [hbm, hbm],
-        out_specs=(hbm, hbm, hbm) + (vm if remote else hbm,) * 3,
+        out_shape=(sd((rows, D), bf), sd((rows, D), bf), sd((slots * PAIRS, 2, SL, SL), bf))
+        + tuple(sd(s, f32) if remote else sd((2,) + u + s, bf) for u, s in zip(leads, shapes)),
+        in_specs=[pl.BlockSpec(memory_space=pltpu.SMEM)] + [vm if remote else hbm] * len(pieces) + [hbm, hbm],
+        out_specs=(hbm, hbm, hbm) + (vm if remote else hbm,) * 4,
         scratch_shapes=scratch,
         compiler_params=pltpu.CompilerParams(**params),
     )(lengths, *pieces, tokens, cotangent)
 
 
-def on_device(cut, remote, tokens, lengths, qkv_weight, out_weight, ffn_in_weight, ffn_out_weight, biases, gains, cotangent):
+def finish(cut, qa, qb, ow, fw, out, gx, g_qkv, g_in, g_out, g_bias, g_gain, g_wo, out2, gx2, SC):
+    r, b = cut.r, cut.b
+    out2[...] = out[...]
+    gx2[...] = gx[...]
+
+    @pl.when(pl.program_id(0) == 0)
+    def _():
+        g_qkv[...] = jnp.concatenate([qa[:, :GW], qa[:, GW:], qb[:, :GW]], 0)
+        g_wo[...] = ow[...]
+        for g in range(GROUPS):
+            g_in[g] = fw[0, :, g * b:(g + 1) * b]
+            g_out[g] = fw[1, :, g * b:(g + 1) * b]
+        SC[...] = jnp.zeros_like(SC)
+        SC[0:r, :] = qb[:, 128:]
+        small = SC[...].T
+        g_bias[...] = small[64:74, 0:r]
+        g_gain[...] = small[74:76, 0:r]
+
+
+def run_finish(cut, parts, out, gx):
+    rows = out.shape[0]
     r, a, b = cut.r, cut.a, cut.b
-    q_piece = jnp.concatenate(
-        [qkv_weight.reshape(3, r, GW).transpose(1, 0, 2).reshape(r, 3 * GW), biases.T, gains.T, jnp.zeros((r, 52), bf)], axis=1)
-    i_piece = jnp.stack([ffn_in_weight.transpose(1, 0, 2).reshape(a, GROUPS * b), ffn_out_weight.transpose(2, 0, 1).reshape(a, GROUPS * b)])
-    out, gx, _, sq, so, si = run_layer(cut, remote, lengths, (q_piece, out_weight, i_piece), tokens, cotangent)
-    g_qkv = sq[:, :3 * GW].reshape(r, 3, GW).transpose(1, 0, 2).reshape(3 * r, GW)
-    g_in = si[0].reshape(a, GROUPS, b).transpose(1, 0, 2)
-    g_out = si[1].reshape(a, GROUPS, b).transpose(1, 2, 0)
-    return out, gx, g_qkv, so, g_in, g_out, sq[:, 576:586].T, sq[:, 586:588].T
+    steps = 2
+    sd = jax.ShapeDtypeStruct
+    tile = pl.BlockSpec((rows // steps, D), lambda i: (i, 0))
+
+    def whole(shape):
+        return pl.BlockSpec(shape, lambda i: (0,) * len(shape))
+
+    small = ((3 * r, GW), (GROUPS, a, b), (GROUPS, a, b), (10, r), (2, r), (r, D))
+    return pl.pallas_call(
+        functools.partial(finish, cut),
+        grid=(steps,),
+        out_shape=tuple(sd(s, f32) for s in small) + (sd((rows, D), bf),) * 2,
+        in_specs=[whole(p.shape) for p in parts] + [tile, tile],
+        out_specs=tuple(whole(s) for s in small) + (tile, tile),
+        scratch_shapes=[pltpu.VMEM((128, 128), f32)],
+    )(*parts, out, gx)
+
+
+def on_device(cut, tokens, lengths, qkv_weight, out_weight, ffn_in_weight, ffn_out_weight, biases, gains, cotangent):
+    pieces = (qkv_weight, out_weight, ffn_in_weight, jnp.swapaxes(ffn_out_weight, 1, 2), biases, gains)
+    out, gx, _, *parts = run_layer(cut, True, lengths, pieces, tokens, cotangent)
+    g_qkv, g_in, g_out, g_bias, g_gain, g_wo, out, gx = run_finish(cut, parts, out, gx)
+    return out, gx, g_qkv, g_wo, g_in, jnp.swapaxes(g_out, 1, 2), g_bias, g_gain
 
 
 def solution(mesh):
     both = ("dp", "ffn")
     P = PartitionSpec
     return jax.shard_map(
-        functools.partial(on_device, Cut(2, mesh.shape["dp"] // 2, mesh.shape["ffn"]), True),
+        functools.partial(on_device, Cut(mesh.shape["dp"] // 2, mesh.shape["ffn"])),
         mesh=mesh,
         in_specs=(P(both, None), P(both), P(both, None), P(both, None), P(None, "dp", "ffn"),
                   P(None, "ffn", "dp"), P(None, both), P(None, both), P(both, None)),

time: 152 us -> 121 us (0.80)
  local copies, waits for them, and re-layouts: 16.1 us -> 0 us
  Pallas kernels: 133 us -> 120 us
    pallas_call x1, Pallas kernels: 133 us -> 115 us  [run_layer(): pl.pallas_call(functools.partial(layer, cut, remote), out_shape=(sd((rows...]
    unnamed x11 -> x0, local copies, waits for them, and re-layouts: 8.25 us -> none
    transpose x6 -> x0, local copies, waits for them, and re-layouts: 4.56 us -> none  [the longest x2 1.56 us: on_device(): return (out, gx, g_qkv, so, g_in, g_out, sq[:, 576:586].T, sq[:, 586:588].T)]
    pallas_call x0 -> x1, Pallas kernels: none -> 4.3 us  [run_finish(): pl.pallas_call(functools.partial(finish, cut), grid=(steps,), out_shape=t...]
    reshape x3 -> x0, local copies, waits for them, and re-layouts: 1.81 us -> none  [the longest x1 0.92 us: on_device(): sq[:, :3 * GW].reshape(r, 3, GW).transpose(1, 0, 2).reshape(3 * r, GW)]
where the time goes in v2:
time: 121 us; the launch traced here: 120 us
  Pallas kernels  120 us (99%)
    pallas_call x1, Pallas kernels, run_layer(): pl.pallas_call(functools.partial(layer, cut, remote), out_shape=(sd((rows...  115 us
    pallas_call x1, Pallas kernels, run_finish(): pl.pallas_call(functools.partial(finish, cut), grid=(steps,), out_shape=t...  4.3 us

profile of v2, /device:TPU:0, one launch (start us, length us, event | category | flops | bytes accessed | tf_op | source)
XLA Modules:
  0.0 120.4 jit_solution(93309461828555600)
XLA Ops:
  0.6 115.5 %shard_map.152 = (bf16[1536,768]{1,0:T(8,128)(2,1)}, bf16[1536,768]{1,0:T(8,128)(2,1)}, bf16[18,2,512,512]{3,2,1,0:T(8,128)(2,1)}, f32[24,384]{1,0:T(8,128)}, f3...) custom-call(s32[3]{0:T(128)} %length.1, bf16[72,192]{1,0:T(8,128)(2,1)} %refs_0_.1, ...), custom_call_target="tpu_custom_call" | custom-call | tf_op jit(solution)/shard_map/pallas_call | solution.py:597
  116.1 4.3 %shard_map.153 = (f32[72,192]{1,0:T(8,128)}, f32[4,24,192]{2,1,0:T(8,128)}, f32[4,24,192]{2,1,0:T(8,128)}, f32[10,24]{1,0:T(8,128)}, f32[2,24]{1,0:T(2,128)}, /*...) custom-call(f32[24,384]{1,0:T(8,128)} %get-tuple-element.22.qa, ...), custom_call_target="tpu_custom_call" | custom-call | tf_op jit(solution)/shard_map/pallas_call | solution.py:638

commit v3 on v2

--- a/solution.py
+++ b/solution.py
@@ -12,6 +12,7 @@
 SL, D, HEADS, GROUPS, GW, GU = 512, 768, 12, 4, 192, 768
 PAIRS = D // 128
 R = 256
+UP = 2
 MESH = pl.DeviceIdType.MESH
 
 
@@ -45,17 +46,8 @@
     return jnp.where(lane < 64, t, z), jnp.where(lane < 64, z, t)
 
 
-def colsum(x):
-    return jnp.sum(x, axis=0, keepdims=True)
-
-
 def rowsum(x):
     return jnp.sum(x, axis=1, keepdims=True)
-
-
-def gelu_pair(u):
-    c = 0.5 + 0.5 * lax.erf(u * 0.7071067811865476)
-    return u * c, c + (0.3989422804014327 * u) * jnp.exp((-0.5) * (u * u))
 
 
 def ln_fwd(r):
@@ -136,46 +128,107 @@
     V[rows, cols] = jnp.concatenate(dv, 0).T.astype(bf)
 
 
-def middle(i, tok, WO, WI, WT, bias, CTX, DC, DR, OB, G1, G2, G3, GB, AB, SLP, XH, H1B, F):
-    rows = rows_of(i, R)
-    ctxb = CTX[rows, :].astype(bf)
-    xh1, inv1 = ln_fwd(nn(ctxb, WO[...]) + bias[6:7, :] + tok[rows, :].astype(f32))
-    XH[...] = xh1
-    h1 = xh1 * bias[10:11, :] + bias[7:8, :]
-    H1B[...] = h1.astype(bf)
-    F[...] = h1 + bias[8:9, :]
+CH = 32
+
+
+def fold(x):
+    return jnp.sum(x.reshape(-1, 8, x.shape[-1]), axis=0)
+
+
+def gelu_pair(u):
+    c = 1.0 + lax.erf(u * 0.7071067811865476)
+    return u * c, c + (0.7978845608028654 * u) * jnp.exp2((-0.7213475204444817 * u) * u)
+
+
+def tile(i, tok, WO, WI, WT, bias, CTX, DC, DR, OB, GB, AB, SLP, H1B, DB, DA, XH, F, INV):
+    r0 = pl.multiple_of(i * R, R)
+    rows = pl.ds(r0, R)
+    parts = [(slice(k, k + CH), pl.ds(r0 + k, CH)) for k in range(0, R, CH)]
+    y = nn(CTX[rows, :].astype(bf), WO[...])
+    for here, there in parts:
+        xh1, inv1 = ln_fwd(y[here] + bias[6:7, :] + tok[there, :].astype(f32))
+        XH[here, :] = xh1
+        INV[here, :] = jnp.broadcast_to(inv1, (CH, 128))
+        h1 = xh1 * bias[10:11, :] + bias[7:8, :]
+        H1B[here, :] = h1.astype(bf)
+        F[here, :] = h1 + bias[8:9, :]
+        yield 1
     for g in range(GROUPS):
         w = slice(win(g), win(g) + 256)
-        a, slope = gelu_pair(nn(H1B[:, w], WI[g]) + bias[g:g + 1, :])
-        ab = a.astype(bf)
-        AB[g] = ab
-        SLP[g] = slope.astype(bf)
-        F[:, w] += nt(ab, WT[g])
-    xh2, inv2 = ln_fwd(F[...])
-    OB[...] = (xh2 * bias[11:12, :] + bias[9:10, :]).astype(bf)
-    gy = DC[rows, :].astype(f32)
-    GB[11:12, :] += colsum(gy * xh2)
-    GB[9:10, :] += colsum(gy)
-    dr2 = ln_bwd(gy, xh2, inv2, bias[11:12, :])
-    dfb = dr2.astype(bf)
-    GB[8:9, :] += colsum(dfb.astype(f32))
-    F[...] = dr2
+        AB[g], SLP[g] = gelu_pair((nn(H1B[:, w], WI[g]) + bias[g:g + 1, :]).astype(bf))
+        F[:, w] += nt(AB[g], WT[g])
+        yield 0
+    sums = [0.0, 0.0, 0.0]
+    for here, there in parts:
+        xh2, inv2 = ln_fwd(F[here, :])
+        OB[here, :] = (xh2 * bias[11:12, :] + bias[9:10, :]).astype(bf)
+        gy = DC[there, :].astype(f32)
+        dr2 = ln_bwd(gy, xh2, inv2, bias[11:12, :])
+        F[here, :] = dr2
+        DB[here, :] = dr2.astype(bf)
+        sums = [s + fold(x) for s, x in zip(sums, (gy * xh2, gy, dr2))]
+        yield 1
+    for k, s in zip((11, 9, 8), sums):
+        GB[k] += s
     for g in range(GROUPS):
         w = slice(win(g), win(g) + 256)
-        o = off(g)
-        dub = (nn(dfb[:, w], WT[g]) * SLP[g].astype(f32)).astype(bf)
-        F[:, w] += nt(dub, WI[g])
-        GB[g:g + 1, :] += colsum(dub.astype(f32))
-        G1[g] += tn(H1B[:, w], dub)[o:o + GW]
-        G2[g] += tn(dfb[:, w], AB[g])[o:o + GW]
-    xh1, dh1 = XH[...], F[...]
-    GB[10:11, :] += colsum(dh1 * xh1)
-    GB[7:8, :] += colsum(dh1)
-    dab = ln_bwd(dh1, xh1, inv1, bias[10:11, :]).astype(bf)
-    GB[6:7, :] += colsum(dab.astype(f32))
-    G3[...] += tn(ctxb, dab)
-    DC[rows, :] = (nt(dab, WO[...]) * DR[rows, :].astype(f32)).astype(bf)
-    DR[rows, :] = dab
+        SLP[g] = nn(DB[:, w], WT[g]).astype(bf) * SLP[g]
+        F[:, w] += nt(SLP[g], WI[g])
+        yield 0
+    sums = [0.0, 0.0, 0.0]
+    for here, there in parts:
+        xh1, dh1 = XH[here, :], F[here, :]
+        dr1 = ln_bwd(dh1, xh1, INV[here, 0:1], bias[10:11, :])
+        DA[here, :] = dr1.astype(bf)
+        sums = [s + fold(x) for s, x in zip(sums, (dh1 * xh1, dh1, dr1))]
+        yield 1
+    for k, s in zip((10, 7, 6), sums):
+        GB[k] += s
+    y = nt(DA[...], WO[...])
+    for here, there in parts:
+        DC[there, :] = (y[here] * DR[there, :].astype(f32)).astype(bf)
+    DR[rows, :] = DA[...]
+    yield 0
+
+
+def weights(i, CTX, G1, G2, G3, GB, AB, SLP, H1B, DB, DA):
+    lane = lax.broadcasted_iota(jnp.int32, (R, 256), 1)
+    rows = rows_of(i, R)
+    for k in range(0, D, 256):
+        G3[k:k + 256, :] += tn(CTX[rows, k:k + 256].astype(bf), DA[...])
+        yield
+    for g in range(GROUPS):
+        w = slice(win(g), win(g) + 256)
+        o, z = off(g), 0 if off(g) else GW
+        mine = jnp.where((lane >= o) & (lane < o + GW), H1B[:, w], jnp.ones((R, 256), bf))
+        t = tn(mine, SLP[g])
+        G1[g] += t[o:o + GW]
+        GB[g, 0:1, :] += t[z:z + 1]
+        yield
+        G2[g] += tn(DB[:, w], AB[g])[o:o + GW]
+        yield
+
+
+PER = 0.5
+
+
+def weave(main, side):
+    credit = 0.0
+    for kind in main:
+        credit += PER * kind
+        while credit >= 1:
+            credit -= 1
+            next(side, None)
+    for _ in side:
+        pass
+
+
+def middle(i, tok, WO, WI, WT, bias, CTX, DC, DR, OB, G1, G2, G3, GB, AB, SLP, H1B, DB, DA, XH, F, INV):
+    for u in range(2):
+        now, last = 2 * i + u, jnp.maximum(2 * i + u - 1, 0)
+        v = 1 - u
+        weave(tile(now, tok, WO, WI, WT, bias, CTX, DC, DR, OB.at[u * R:(u + 1) * R], GB, AB.at[u], SLP.at[u], H1B.at[u], DB.at[u], DA.at[u], XH, F, INV),
+              weights(last, CTX, G1, G2, G3, GB, AB.at[v], SLP.at[v], H1B.at[v], DB.at[v], DA.at[v]))
 
 
 def qkv_grads(tok, Q, K, V, G1, GB, s):
@@ -184,8 +237,8 @@
         w = slice(win(g), win(g) + 256)
         d3 = jnp.concatenate([Q[rows, w], K[rows, w], V[rows, w]], axis=1)
         G1[g] += tn(tok[rows, w], d3)[off(g):off(g) + GW]
-    GB[4:5, :] += colsum(Q[rows, :].astype(f32))
-    GB[5:6, :] += colsum(V[rows, :].astype(f32))
+    GB[4] += fold(Q[rows, :].astype(f32))
+    GB[5] += fold(V[rows, :].astype(f32))
 
 
 def token_grads(wq, Q, K, V, DR, s):
@@ -202,7 +255,8 @@
 
 
 QA, QB, OW, FW = range(4)
-ORDER = ("qf", "fq", "fq", "qf")
+GATHER = ("qf", "qf", "fq", "qf")
+SCATTER = ("qf", "fq", "fq", "qf")
 
 
 class Cut:
@@ -214,12 +268,14 @@
         self.shapes = ((self.r, 2 * GW), (self.r, 256), (self.r, D), (2, self.a, GROUPS * self.b))
 
     def lead(self, i):
-        return (self.nq, self.nf) if ORDER[i] == "qf" else (self.nf, self.nq)
-
-    def at(self, i, d):
+        return (self.nq, self.nf) if SCATTER[i] == "qf" else (self.nf, self.nq)
+
+    def place(self, order, q, f):
+        return q * self.nf + f if order == "qf" else f * self.nq + q
+
+    def at(self, order, d):
         dp, f = divmod(d, self.nf)
-        c, q = dp % 2, dp // 2
-        return (c, q, f) if ORDER[i] == "qf" else (c, f, q)
+        return dp % 2, self.place(order, dp // 2, f)
 
 
 def put_pieces(cut, at, qkv, wo, wi, wt, biases, gains, SC, G):
@@ -244,19 +300,19 @@
             for i in range(GW // r):
                 d, j = divmod((D * p + GW * g) // r + i, 3)
                 if j < 2:
-                    parts.append(G[QA][cut.at(QA, d)].astype(f32)[:, GW * j:GW * (j + 1)])
+                    parts.append(G[QA][cut.at(GATHER[QA], d)].astype(f32)[:, GW * j:GW * (j + 1)])
                 else:
-                    parts.append(G[QB][cut.at(QB, d)].astype(f32)[:, :GW])
+                    parts.append(G[QB][cut.at(GATHER[QB], d)].astype(f32)[:, :GW])
             o = off(g)
             WQ[g, o:o + GW, 256 * p + o:256 * p + o + GW] = jnp.concatenate(parts, 0).astype(bf)
-    small = jnp.concatenate([G[QB][cut.at(QB, d)][:, 128:].astype(f32) for d in range(cut.n)], 0)
+    small = jnp.concatenate([G[QB][cut.at(GATHER[QB], d)][:, 128:].astype(f32) for d in range(cut.n)], 0)
     SM[...] = small.T[64:80]
 
 
 def unpack_o(cut, G, WO):
     per = GW // cut.r
     for i in range(D // GW):
-        rows = [G[OW][cut.at(OW, d)].astype(f32) for d in range(per * i, per * i + per)]
+        rows = [G[OW][cut.at(GATHER[OW], d)].astype(f32) for d in range(per * i, per * i + per)]
         WO[GW * i:GW * (i + 1), :] = jnp.concatenate(rows, 0).astype(bf)
 
 
@@ -270,13 +326,14 @@
             cols = []
             for f in range(cut.nf):
                 cols.append(jnp.concatenate(
-                    [G[FW][cut.at(FW, dp * cut.nf + f)][k].astype(f32)[:, g * b:(g + 1) * b] for dp in range(2 * cut.nq)], 0))
-            W[g, o:o + GW] = jnp.concatenate(cols, 1).astype(bf)
+                    [G[FW][cut.at(GATHER[FW], dp * cut.nf + f)][k].astype(f32)[:, g * b:(g + 1) * b] for dp in range(2 * cut.nq)], 0))
+            w = jnp.concatenate(cols, 1)
+            W[g, o:o + GW] = (0.5 * w if k else w).astype(bf)
 
 
 def pack_o(cut, G3, G):
     for d in range(cut.n):
-        G[OW][cut.at(OW, d)] = G3[cut.r * d:cut.r * (d + 1), :].astype(bf)
+        G[OW][cut.at(SCATTER[OW], d)] = G3[cut.r * d:cut.r * (d + 1), :].astype(bf)
 
 
 def pack_f(cut, G1, G2, G):
@@ -284,13 +341,13 @@
     for k, grad in enumerate((G1, G2)):
         for dp in range(2 * cut.nq):
             for f in range(cut.nf):
-                G[FW][cut.at(FW, dp * cut.nf + f) + (k,)] = jnp.concatenate(
-                    [grad[g, a * dp:a * (dp + 1), b * f:b * (f + 1)] for g in range(GROUPS)], 1).astype(bf)
+                t = jnp.concatenate([grad[g, a * dp:a * (dp + 1), b * f:b * (f + 1)] for g in range(GROUPS)], 1)
+                G[FW][cut.at(SCATTER[FW], dp * cut.nf + f) + (k,)] = (0.5 * t if k else t).astype(bf)
 
 
 def pack_q(cut, G1, GB, G):
     r = cut.r
-    small = jnp.concatenate([jnp.zeros((64, D), f32), GB[...], jnp.zeros((48, D), f32)], 0).T
+    small = jnp.concatenate([jnp.zeros((64, D), f32), jnp.sum(GB[...], axis=1), jnp.zeros((48, D), f32)], 0).T
     for d in range(cut.n):
         parts = []
         for j in range(3):
@@ -298,8 +355,8 @@
             g, i = divmod(rest, GW)
             c = 256 * p + off(g)
             parts.append(G1[g, i:i + r, c:c + GW])
-        G[QA][cut.at(QA, d)] = jnp.concatenate(parts[:2], 1).astype(bf)
-        G[QB][cut.at(QB, d)] = jnp.concatenate([parts[2], small[r * d:r * (d + 1), 64:]], 1).astype(bf)
+        G[QA][cut.at(SCATTER[QA], d)] = jnp.concatenate(parts[:2], 1).astype(bf)
+        G[QB][cut.at(SCATTER[QB], d)] = jnp.concatenate([parts[2], small[r * d:r * (d + 1), 64:]], 1).astype(bf)
 
 
 class Links:
@@ -317,7 +374,7 @@
         self.per = nf + nq - 1
 
     def at(self, i):
-        return (self.c, self.q, self.f) if ORDER[i] == "qf" else (self.c, self.f, self.q)
+        return self.c, self.cut.place(GATHER[i], self.q, self.f)
 
     def greet(self):
         barrier = pltpu.get_barrier_semaphore()
@@ -333,37 +390,42 @@
 
     def gather(self, stage, i, G):
         base, c = i * self.per, self.c
-        (u, us, to_u), (v, vs, to_v) = (self.axis[x] for x in ORDER[i])
+        (u, us, to_u), (v, vs, to_v) = (self.axis[x] for x in GATHER[i])
+        size = len(vs) + 1
         if stage == 0:
-            return [self.copy(G.at[c, u, v], G.at[c, u, v], base + k, to_v[k]) for k in range(len(vs))]
+            mine = G.at[c, u * size + v]
+            return [self.copy(mine, mine, base + k, to_v[k]) for k in range(len(vs))]
         base += len(vs)
         if stage == 1:
-            return [self.copy(G.at[c, u], G.at[c, u], base + k, to_u[k]) for k in range(len(us))]
+            mine = G.at[c, pl.ds(u * size, size)]
+            return [self.copy(mine, mine, base + k, to_u[k]) for k in range(len(us))]
         return [self.copy(G.at[c], G.at[c], base + len(us), self.twin)]
 
     def scatter(self, stage, i, G, RC, RU, Z, RV):
         base, c = (4 + i) * self.per, self.c
-        (u, us, to_u), (v, vs, to_v) = (self.axis[x] for x in ORDER[i])
+        (u, us, to_u), (v, vs, to_v) = (self.axis[x] for x in SCATTER[i])
+        size = len(vs) + 1
         if stage == 0:
             return [self.copy(G.at[1 - c], RC, base, self.twin)]
         base += 1
         if stage == 1:
-            return [self.copy(G.at[c, us[k]], RU.at[k], base + k, to_u[k]) for k in range(len(us))]
+            return [self.copy(G.at[c, pl.ds(us[k] * size, size)], RU.at[k], base + k, to_u[k]) for k in range(len(us))]
         base += len(us)
         return [self.copy(Z.at[vs[k]], RV.at[k], base + k, to_v[k]) for k in range(len(vs))]
 
     def add_twin(self, i, G, RC, RU, Z, RV):
-        for u in range(G.shape[1]):
-            G[self.c, u] = (G[self.c, u].astype(f32) + RC[u].astype(f32)).astype(bf)
+        for k in range(RC.shape[0]):
+            G[self.c, k] = (G[self.c, k].astype(f32) + RC[k].astype(f32)).astype(bf)
 
     def add_u(self, i, G, RC, RU, Z, RV):
-        total = G[self.c, self.axis[ORDER[i][0]][0]].astype(f32)
+        size = Z.shape[0]
+        total = G[self.c, pl.ds(self.axis[SCATTER[i][0]][0] * size, size)].astype(f32)
         for k in range(RU.shape[0]):
             total = total + RU[k].astype(f32)
         Z[...] = total.astype(bf)
 
     def add_v(self, i, G, RC, RU, Z, RV):
-        total = Z[self.axis[ORDER[i][1]][0]].astype(f32)
+        total = Z[self.axis[SCATTER[i][1]][0]].astype(f32)
         for k in range(RV.shape[0]):
             total = total + RV[k].astype(f32)
         return total
@@ -394,10 +456,10 @@
     if remote:
         parts, refs = [refs[4 * k:4 * k + 4] for k in range(4)], refs[16:]
         RC, RU, Z, RV = parts
-    G1, G2, G3, GB, SC, AB, SLP, XH, H1B, F, OB, PB, in_sem, p_sem, o_sem, x_sem = refs[:16]
+    G1, G2, G3, GB, SC, AB, SLP, H1B, DB, DA, XH, F, INV, OB, PB, in_sem, p_sem, o_sem, x_sem = refs[:19]
     slots = tok.shape[0] // SL
-    nmid = tok.shape[0] // R
-    links = Links(cut, *refs[16:]) if remote else None
+    nmid = tok.shape[0] // (2 * R)
+    links = Links(cut, *refs[19:]) if remote else None
 
     def gather(stage, which):
         return sum((links.gather(stage, i, G[i]) for i in which), [])
@@ -425,15 +487,19 @@
     if remote:
         arrive(gather(0, early))
         start(gather(1, early))
+        start(gather(0, (FW,)))
         arrive(gather(1, early))
         start(gather(2, early))
-        start(gather(0, late))
+        start(gather(0, (OW,)))
         arrive(gather(2, early))
     unpack_q(cut, G, WQ, SM)
+    if remote:
+        arrive(gather(0, late))
+        start(gather(1, late))
     loads[0].wait()
     lax.fori_loop(0, slots, lambda s, x: (project(tok, WQ, SM, Q, K, V, s), x)[1], 0)
 
-    steps = slots * PAIRS // 2
+    steps = slots * PAIRS // UP
 
     def to_hbm(i, slot):
         return pltpu.make_async_copy(PB.at[slot], phbm.at[i], p_sem.at[slot])
@@ -443,58 +509,58 @@
 
         @pl.when(i >= 2)
         def _():
-            for u in range(2):
-                to_hbm(2 * i + u, 2 * half + u).wait()
+            for u in range(UP):
+                to_hbm(UP * i + u, UP * half + u).wait()
 
         if remote:
-            @pl.when(i == 1)
+            @pl.when(i == steps - 2)
             def _():
-                arrive(gather(0, late))
-                start(gather(1, late))
-
-        for u in range(2):
-            pair = 2 * i + u
+                arrive(gather(1, late))
+                start(gather(2, late))
+
+        for u in range(UP):
+            pair = UP * i + u
             s = lax.div(pair, PAIRS)
             lane = lax.broadcasted_iota(jnp.int32, (1, SL), 1)
             maskrow = jnp.where(lane < length[s], 0.0, NEG)
-            attend(Q, K, V, PB.at[2 * half + u], CTX, DR, maskrow, s, lax.rem(pair, PAIRS))
-        for u in range(2):
-            to_hbm(2 * i + u, 2 * half + u).start()
+            attend(Q, K, V, PB.at[UP * half + u], CTX, DR, maskrow, s, lax.rem(pair, PAIRS))
+        for u in range(UP):
+            to_hbm(UP * i + u, UP * half + u).start()
         return x
 
     lax.fori_loop(0, steps, forward, 0)
     if remote:
-        arrive(gather(1, late))
-        start(gather(2, late))
         arrive(gather(2, late))
     unpack_o(cut, G, WO)
     unpack_f(cut, G, WI, WT)
     loads[1].wait()
     for i in range(max(0, steps - 2), steps):
-        for u in range(2):
-            to_hbm(2 * i + u, 2 * (i % 2) + u).wait()
+        for u in range(UP):
+            to_hbm(UP * i + u, UP * (i % 2) + u).wait()
 
     def from_hbm(i, slot):
         return pltpu.make_async_copy(phbm.at[i], PB.at[slot], p_sem.at[slot])
 
-    for u in range(2):
+    for u in range(UP):
         from_hbm(u, u).start()
 
     def out_copy(i, slot):
-        return pltpu.make_async_copy(OB.at[slot], out.at[rows_of(i, R), :], o_sem.at[slot])
+        return pltpu.make_async_copy(OB.at[slot], out.at[rows_of(i, 2 * R), :], o_sem.at[slot])
 
     def mid(i, x):
-        slot = lax.rem(i, 2)
-
-        @pl.when(i >= 2)
+        @pl.when(i >= 1)
         def _():
-            out_copy(i, slot).wait()
-
-        middle(i, tok, WO, WI, WT, SM, CTX, DC, DR, OB.at[slot], G1, G2, G3, GB, AB, SLP, XH, H1B, F)
-        out_copy(i, slot).start()
+            out_copy(i, 0).wait()
+
+        middle(i, tok, WO, WI, WT, SM, CTX, DC, DR, OB.at[0], G1, G2, G3, GB, AB, SLP, H1B, DB, DA, XH, F, INV)
+        out_copy(i, 0).start()
         return x
 
+    for ref in (AB, SLP, H1B, DB, DA):
+        ref[1] = jnp.zeros(ref.shape[1:], bf)
     lax.fori_loop(0, nmid, mid, 0)
+    for _ in weights(2 * nmid - 1, CTX, G1, G2, G3, GB, AB.at[1], SLP.at[1], H1B.at[1], DB.at[1], DA.at[1]):
+        pass
     if remote:
         sent(sum((gather(stage, early + late) for stage in range(3)), []))
     pack_o(cut, G3, G)
@@ -508,30 +574,28 @@
 
         @pl.when(i + 1 < steps)
         def _():
-            for u in range(2):
-                from_hbm(2 * i + 2 + u, 2 - 2 * half + u).start()
+            for u in range(UP):
+                from_hbm(UP * i + UP + u, UP - UP * half + u).start()
 
         if remote:
-            @pl.when(i == 1)
+            @pl.when(i == 2)
             def _():
                 arrive(scatter(0, late))
                 add(links.add_twin, late)
                 start(scatter(1, late))
 
-            @pl.when(i == steps - 1)
-            def _():
-                arrive(scatter(1, late))
-                add(links.add_u, late)
-                start(scatter(2, late))
-
-        for u in range(2):
-            from_hbm(2 * i + u, 2 * half + u).wait()
-        for u in range(2):
-            pair = 2 * i + u
-            attend_back(Q, K, V, PB.at[2 * half + u], CTX, DC, lax.div(pair, PAIRS), lax.rem(pair, PAIRS))
+        for u in range(UP):
+            from_hbm(UP * i + u, UP * half + u).wait()
+        for u in range(UP):
+            pair = UP * i + u
+            attend_back(Q, K, V, PB.at[UP * half + u], CTX, DC, lax.div(pair, PAIRS), lax.rem(pair, PAIRS))
         return x
 
     lax.fori_loop(0, steps, backward, 0)
+    if remote:
+        arrive(scatter(1, late))
+        add(links.add_u, late)
+        start(scatter(2, late))
     lax.fori_loop(0, slots, lambda s, x: (qkv_grads(tok, Q, K, V, G1, GB, s), x)[1], 0)
     pack_q(cut, G1, GB, G)
     if remote:
@@ -540,7 +604,7 @@
     def gx_copy(s):
         return pltpu.make_async_copy(DR.at[rows_of(s, SL), :], gx.at[rows_of(s, SL), :], x_sem.at[s])
 
-    def last(s, x):
+    def final(s, x):
         if remote:
             @pl.when(s == 1)
             def _():
@@ -551,7 +615,7 @@
         gx_copy(s).start()
         return x
 
-    lax.fori_loop(0, slots, last, 0)
+    lax.fori_loop(0, slots, final, 0)
     if remote:
         arrive(scatter(2, late))
         for i, total in zip(late, add(links.add_v, late)):
@@ -562,12 +626,11 @@
         arrive(scatter(2, early))
         for i, total in zip(early, add(links.add_v, early)):
             results[i][...] = total
-        sent(sum((scatter(stage, early + late) for stage in range(3)), []))
+        sent(sum((scatter(stage, late + early) for stage in range(3)), []))
     else:
         for src, dst in zip(G, results):
             pltpu.sync_copy(src, dst)
-    for i in range(max(0, nmid - 2), nmid):
-        out_copy(i, i % 2).wait()
+    out_copy(nmid - 1, 0).wait()
     for s in range(slots):
         gx_copy(s).wait()
 
@@ -580,15 +643,17 @@
     shapes, leads = cut.shapes, [cut.lead(i) for i in range(4)]
     scratch = [vmem((rows, D), bf)] * 5 + [vmem((rows, D), f32), vmem((rows, D), bf)]
     scratch += [vmem((GROUPS, 256, 768), bf), vmem((D, D), bf), vmem((GROUPS, 256, GU), bf), vmem((GROUPS, 256, GU), bf), vmem((16, D), f32)]
-    scratch += [vmem((2,) + u + s, bf) for u, s in zip(leads, shapes)]
-    if remote:
-        scratch += [vmem(u + s, bf) for u, s in zip(leads, shapes)]
-        scratch += [vmem((u[0] - 1, u[1]) + s, bf) for u, s in zip(leads, shapes)]
-        scratch += [vmem(u[1:] + s, bf) for u, s in zip(leads, shapes)]
-        scratch += [vmem((u[1] - 1,) + s, bf) for u, s in zip(leads, shapes)]
-    scratch += [vmem((GROUPS, GW, GU), f32)] * 2 + [vmem((D, D), f32), vmem((16, D), f32), vmem((128, 128), f32)]
-    scratch += [vmem((GROUPS, R, GU), bf)] * 2 + [vmem((R, D), f32), vmem((R, D), bf), vmem((R, D), f32), vmem((2, R, D), bf)]
-    scratch += [vmem((4, 2, SL, SL), bf), dma((2,)), dma((4,)), dma((2,)), dma((slots,))]
+    scratch += [vmem((2, u[0] * u[1]) + s, bf) for u, s in zip(leads, shapes)]
+    if remote:
+        back = list(zip(leads, shapes))
+        scratch += [vmem((u[0] * u[1],) + s, bf) for u, s in back]
+        scratch += [vmem((u[0] - 1, u[1]) + s, bf) for u, s in back]
+        scratch += [vmem(u[1:] + s, bf) for u, s in back]
+        scratch += [vmem((u[1] - 1,) + s, bf) for u, s in back]
+    scratch += [vmem((GROUPS, GW, GU), f32)] * 2 + [vmem((D, D), f32), vmem((16, 8, D), f32), vmem((128, 128), f32)]
+    scratch += [vmem((2, GROUPS, R, GU), bf)] * 2 + [vmem((2, R, D), bf)] * 3 + [vmem((R, D), f32)] * 2
+    scratch += [vmem((R, 128), f32), vmem((1, 2 * R, D), bf)]
+    scratch += [vmem((2 * UP, 2, SL, SL), bf), dma((2,)), dma((4,)), dma((2,)), dma((slots,))]
     params = dict(vmem_limit_bytes=64 * 1024 * 1024 - 65536)
     if remote:
         count = 8 * (cut.nf + cut.nq - 1)
@@ -597,7 +662,7 @@
     return pl.pallas_call(
         functools.partial(layer, cut, remote),
         out_shape=(sd((rows, D), bf), sd((rows, D), bf), sd((slots * PAIRS, 2, SL, SL), bf))
-        + tuple(sd(s, f32) if remote else sd((2,) + u + s, bf) for u, s in zip(leads, shapes)),
+        + tuple(sd(s, f32) if remote else sd((2, u[0] * u[1]) + s, bf) for u, s in zip(leads, shapes)),
         in_specs=[pl.BlockSpec(memory_space=pltpu.SMEM)] + [vm if remote else hbm] * len(pieces) + [hbm, hbm],
         out_specs=(hbm, hbm, hbm) + (vm if remote else hbm,) * 4,
         scratch_shapes=scratch,

time: 121 us -> 115 us (0.950)
  Pallas kernels: 120 us -> 114 us
    pallas_call x1, Pallas kernels: 115 us -> 110 us  [run_layer(): pl.pallas_call(functools.partial(layer, cut, remote), out_shape=(sd((rows...]
where the time goes in v3:
time: 115 us
  Pallas kernels  114 us (99%)
    pallas_call x1, Pallas kernels, run_layer(): pl.pallas_call(functools.partial(layer, cut, remote), out_shape=(sd((rows...  110 us
    pallas_call x1, Pallas kernels, run_finish(): pl.pallas_call(functools.partial(finish, cut), grid=(steps,), out_shape=t...  4.3 us

profile of v3, /device:TPU:0, one launch (start us, length us, event | category | flops | bytes accessed | tf_op | source)
XLA Modules:
  0.0 114.8 jit_solution(6388495470421815407)
XLA Ops:
  0.6 109.8 %shard_map.152 = (bf16[1536,768]{1,0:T(8,128)(2,1)}, bf16[1536,768]{1,0:T(8,128)(2,1)}, bf16[18,2,512,512]{3,2,1,0:T(8,128)(2,1)}, f32[24,384]{1,0:T(8,128)}, f3...) custom-call(s32[3]{0:T(128)} %length.1, bf16[72,192]{1,0:T(8,128)(2,1)} %refs_0_.1, ...), custom_call_target="tpu_custom_call" | custom-call | tf_op jit(solution)/shard_map/pallas_call | solution.py:662
  110.5 4.3 %shard_map.153 = (f32[72,192]{1,0:T(8,128)}, f32[4,24,192]{2,1,0:T(8,128)}, f32[4,24,192]{2,1,0:T(8,128)}, f32[10,24]{1,0:T(8,128)}, f32[2,24]{1,0:T(2,128)}, /*...) custom-call(f32[24,384]{1,0:T(8,128)} %get-tuple-element.22.qa, ...), custom_call_target="tpu_custom_call" | custom-call | tf_op jit(solution)/shard_map/pallas_call | solution.py:703

commit v4 on v3

--- a/solution.py
+++ b/solution.py
@@ -12,7 +12,6 @@
 SL, D, HEADS, GROUPS, GW, GU = 512, 768, 12, 4, 192, 768
 PAIRS = D // 128
 R = 256
-UP = 2
 MESH = pl.DeviceIdType.MESH
 
 
@@ -108,7 +107,7 @@
     rows, cols = pl.ds(r0, SL), rows_of(p, 128)
     q, k, v, dc = Q[rows, cols], K[rows, cols], V[rows, cols], DC[rows, cols]
     kcat = jnp.concatenate(halves(k), 0)
-    dss = [[], []]
+    dss, dq = [[], []], []
     for t in range(SL // T):
         rt = pl.ds(r0 + t * T, T)
         dct = dc[t * T:(t + 1) * T]
@@ -119,13 +118,19 @@
             ds = (P[h, t * T:(t + 1) * T].astype(f32) * dp).astype(bf)
             dss[h].append(ds)
             row.append(ds)
-        Q[rt, cols] = (nn(jnp.concatenate(row, 1), kcat) * 0.125).astype(bf)
+        dq.append((nn(jnp.concatenate(row, 1), kcat) * 0.125).astype(bf))
     dk, dv = [], []
     for h in range(2):
         dk.append(tn(q, jnp.concatenate(dss[h], 0))[64 * h:64 * h + 64])
         dv.append(tn(dc, P[h])[64 * h:64 * h + 64])
-    K[rows, cols] = jnp.concatenate(dk, 0).T.astype(bf)
-    V[rows, cols] = jnp.concatenate(dv, 0).T.astype(bf)
+    dk, dv = jnp.concatenate(dk, 0).astype(bf).T, jnp.concatenate(dv, 0).astype(bf).T
+
+    def put():
+        Q[rows, cols] = jnp.concatenate(dq, 0)
+        K[rows, cols] = dk
+        V[rows, cols] = dv
+
+    return put
 
 
 CH = 32
@@ -161,7 +166,9 @@
     sums = [0.0, 0.0, 0.0]
     for here, there in parts:
         xh2, inv2 = ln_fwd(F[here, :])
-        OB[here, :] = (xh2 * bias[11:12, :] + bias[9:10, :]).astype(bf)
+        y = (xh2 * bias[11:12, :] + bias[9:10, :]).astype(bf)
+        OB[0, here, 0:D // 2] = y[:, :D // 2]
+        OB[1, here, 0:D // 2] = y[:, D // 2:]
         gy = DC[there, :].astype(f32)
         dr2 = ln_bwd(gy, xh2, inv2, bias[11:12, :])
         F[here, :] = dr2
@@ -227,18 +234,20 @@
     for u in range(2):
         now, last = 2 * i + u, jnp.maximum(2 * i + u - 1, 0)
         v = 1 - u
-        weave(tile(now, tok, WO, WI, WT, bias, CTX, DC, DR, OB.at[u * R:(u + 1) * R], GB, AB.at[u], SLP.at[u], H1B.at[u], DB.at[u], DA.at[u], XH, F, INV),
+        weave(tile(now, tok, WO, WI, WT, bias, CTX, DC, DR, OB.at[:, u * R:(u + 1) * R], GB, AB.at[u], SLP.at[u], H1B.at[u], DB.at[u], DA.at[u], XH, F, INV),
               weights(last, CTX, G1, G2, G3, GB, AB.at[v], SLP.at[v], H1B.at[v], DB.at[v], DA.at[v]))
 
 
-def qkv_grads(tok, Q, K, V, G1, GB, s):
-    rows = rows_of(s, SL)
+def qkv_grads(tok, Q, K, V, G1, GB):
+    lane = lax.broadcasted_iota(jnp.int32, (tok.shape[0], 256), 1)
     for g in range(GROUPS):
         w = slice(win(g), win(g) + 256)
-        d3 = jnp.concatenate([Q[rows, w], K[rows, w], V[rows, w]], axis=1)
-        G1[g] += tn(tok[rows, w], d3)[off(g):off(g) + GW]
-    GB[4] += fold(Q[rows, :].astype(f32))
-    GB[5] += fold(V[rows, :].astype(f32))
+        o, z = off(g), 0 if off(g) else GW
+        mine = jnp.where((lane >= o) & (lane < o + GW), tok[:, w], jnp.ones_like(tok[:, w]))
+        t = tn(mine, jnp.concatenate([Q[:, w], K[:, w], V[:, w]], axis=1))
+        G1[g] = t[o:o + GW]
+        for k, c in ((4, o), (5, 512 + o)):
+            GB[k, 0:1, GW * g:GW * (g + 1)] = t[z:z + 1, c:c + GW]
 
 
 def token_grads(wq, Q, K, V, DR, s):
@@ -265,6 +274,7 @@
         self.n = 2 * nq * nf
         self.r = D // self.n
         self.a, self.b = GW // (2 * nq), GU // nf
+        self.pairs = 3 if self.r % 8 == 0 else 2
         self.shapes = ((self.r, 2 * GW), (self.r, 256), (self.r, D), (2, self.a, GROUPS * self.b))
 
     def lead(self, i):
@@ -456,10 +466,10 @@
     if remote:
         parts, refs = [refs[4 * k:4 * k + 4] for k in range(4)], refs[16:]
         RC, RU, Z, RV = parts
-    G1, G2, G3, GB, SC, AB, SLP, H1B, DB, DA, XH, F, INV, OB, PB, in_sem, p_sem, o_sem, x_sem = refs[:19]
+    G1, G2, G3, GB, SC, AB, SLP, H1B, DB, DA, XH, F, INV, PB, in_sem, p_sem, o_sem, x_sem = refs[:18]
     slots = tok.shape[0] // SL
     nmid = tok.shape[0] // (2 * R)
-    links = Links(cut, *refs[19:]) if remote else None
+    links = Links(cut, *refs[18:]) if remote else None
 
     def gather(stage, which):
         return sum((links.gather(stage, i, G[i]) for i in which), [])
@@ -499,6 +509,7 @@
     loads[0].wait()
     lax.fori_loop(0, slots, lambda s, x: (project(tok, WQ, SM, Q, K, V, s), x)[1], 0)
 
+    UP = cut.pairs
     steps = slots * PAIRS // UP
 
     def to_hbm(i, slot):
@@ -513,7 +524,7 @@
                 to_hbm(UP * i + u, UP * half + u).wait()
 
         if remote:
-            @pl.when(i == steps - 2)
+            @pl.when(i == steps * 5 // 6)
             def _():
                 arrive(gather(1, late))
                 start(gather(2, late))
@@ -544,16 +555,20 @@
     for u in range(UP):
         from_hbm(u, u).start()
 
-    def out_copy(i, slot):
-        return pltpu.make_async_copy(OB.at[slot], out.at[rows_of(i, 2 * R), :], o_sem.at[slot])
+    OB = PB.at[2 * UP - 1]
+
+    def out_copy(i):
+        return [pltpu.make_async_copy(OB.at[h, :, 0:D // 2], out.at[rows_of(i, 2 * R), h * (D // 2):(h + 1) * (D // 2)], o_sem.at[h])
+                for h in range(2)]
 
     def mid(i, x):
         @pl.when(i >= 1)
         def _():
-            out_copy(i, 0).wait()
-
-        middle(i, tok, WO, WI, WT, SM, CTX, DC, DR, OB.at[0], G1, G2, G3, GB, AB, SLP, H1B, DB, DA, XH, F, INV)
-        out_copy(i, 0).start()
+            for copy in out_copy(i):
+                copy.wait()
+
+        middle(i, tok, WO, WI, WT, SM, CTX, DC, DR, OB, G1, G2, G3, GB, AB, SLP, H1B, DB, DA, XH, F, INV)
+        start(out_copy(i))
         return x
 
     for ref in (AB, SLP, H1B, DB, DA):
@@ -567,7 +582,9 @@
     pack_f(cut, G1, G2, G)
     if remote:
         start(scatter(0, late))
-    G1[...] = jnp.zeros_like(G1)
+
+    for copy in out_copy(nmid - 1):
+        copy.wait()
 
     def backward(i, x):
         half = lax.rem(i, 2)
@@ -578,7 +595,7 @@
                 from_hbm(UP * i + UP + u, UP - UP * half + u).start()
 
         if remote:
-            @pl.when(i == 2)
+            @pl.when(i == steps // 4)
             def _():
                 arrive(scatter(0, late))
                 add(links.add_twin, late)
@@ -586,9 +603,12 @@
 
         for u in range(UP):
             from_hbm(UP * i + u, UP * half + u).wait()
+        puts = []
         for u in range(UP):
             pair = UP * i + u
-            attend_back(Q, K, V, PB.at[UP * half + u], CTX, DC, lax.div(pair, PAIRS), lax.rem(pair, PAIRS))
+            puts.append(attend_back(Q, K, V, PB.at[UP * half + u], CTX, DC, lax.div(pair, PAIRS), lax.rem(pair, PAIRS)))
+        for put in puts:
+            put()
         return x
 
     lax.fori_loop(0, steps, backward, 0)
@@ -596,7 +616,7 @@
         arrive(scatter(1, late))
         add(links.add_u, late)
         start(scatter(2, late))
-    lax.fori_loop(0, slots, lambda s, x: (qkv_grads(tok, Q, K, V, G1, GB, s), x)[1], 0)
+    qkv_grads(tok, Q, K, V, G1, GB)
     pack_q(cut, G1, GB, G)
     if remote:
         start(scatter(0, early))
@@ -630,7 +650,6 @@
     else:
         for src, dst in zip(G, results):
             pltpu.sync_copy(src, dst)
-    out_copy(nmid - 1, 0).wait()
     for s in range(slots):
         gx_copy(s).wait()
 
@@ -652,8 +671,8 @@
         scratch += [vmem((u[1] - 1,) + s, bf) for u, s in back]
     scratch += [vmem((GROUPS, GW, GU), f32)] * 2 + [vmem((D, D), f32), vmem((16, 8, D), f32), vmem((128, 128), f32)]
     scratch += [vmem((2, GROUPS, R, GU), bf)] * 2 + [vmem((2, R, D), bf)] * 3 + [vmem((R, D), f32)] * 2
-    scratch += [vmem((R, 128), f32), vmem((1, 2 * R, D), bf)]
-    scratch += [vmem((2 * UP, 2, SL, SL), bf), dma((2,)), dma((4,)), dma((2,)), dma((slots,))]
+    scratch += [vmem((R, 128), f32)]
+    scratch += [vmem((2 * cut.pairs, 2, SL, SL), bf), dma((2,)), dma((2 * cut.pairs,)), dma((2,)), dma((slots,))]
     params = dict(vmem_limit_bytes=64 * 1024 * 1024 - 65536)
     if remote:
         count = 8 * (cut.nf + cut.nq - 1)

time: 115 us -> 113 us (0.983)
  Pallas kernels: 114 us -> 112 us
    pallas_call x1, Pallas kernels: 110 us -> 108 us  [run_layer(): pl.pallas_call(functools.partial(layer, cut, remote), out_shape=(sd((rows...]
where the time goes in v4:
time: 113 us
  Pallas kernels  112 us (99%)
    pallas_call x1, Pallas kernels, run_layer(): pl.pallas_call(functools.partial(layer, cut, remote), out_shape=(sd((rows...  108 us
    pallas_call x1, Pallas kernels, run_finish(): pl.pallas_call(functools.partial(finish, cut), grid=(steps,), out_shape=t...  4.3 us

profile of v4, /device:TPU:0, one launch (start us, length us, event | category | flops | bytes accessed | tf_op | source)
XLA Modules:
  0.0 113.0 jit_solution(8363971749358338429)
XLA Ops:
  0.6 108.1 %shard_map.152 = (bf16[1536,768]{1,0:T(8,128)(2,1)}, bf16[1536,768]{1,0:T(8,128)(2,1)}, bf16[18,2,512,512]{3,2,1,0:T(8,128)(2,1)}, f32[24,384]{1,0:T(8,128)}, f3...) custom-call(s32[3]{0:T(128)} %length.1, bf16[72,192]{1,0:T(8,128)(2,1)} %refs_0_.1, ...), custom_call_target="tpu_custom_call" | custom-call | tf_op jit(solution)/shard_map/pallas_call | solution.py:681
  108.7 4.3 %shard_map.153 = (f32[72,192]{1,0:T(8,128)}, f32[4,24,192]{2,1,0:T(8,128)}, f32[4,24,192]{2,1,0:T(8,128)}, f32[10,24]{1,0:T(8,128)}, f32[2,24]{1,0:T(2,128)}, /*...) custom-call(f32[24,384]{1,0:T(8,128)} %get-tuple-element.22.qa, ...), custom_call_target="tpu_custom_call" | custom-call | tf_op jit(solution)/shard_map/pallas_call | solution.py:722

commit v5 on v4

--- a/solution.py
+++ b/solution.py
@@ -152,7 +152,8 @@
     y = nn(CTX[rows, :].astype(bf), WO[...])
     for here, there in parts:
         xh1, inv1 = ln_fwd(y[here] + bias[6:7, :] + tok[there, :].astype(f32))
-        XH[here, :] = xh1
+        XH[0, here, 0:D // 2] = xh1[:, :D // 2].astype(bf)
+        XH[1, here, 0:D // 2] = xh1[:, D // 2:].astype(bf)
         INV[here, :] = jnp.broadcast_to(inv1, (CH, 128))
         h1 = xh1 * bias[10:11, :] + bias[7:8, :]
         H1B[here, :] = h1.astype(bf)
@@ -184,7 +185,8 @@
         yield 0
     sums = [0.0, 0.0, 0.0]
     for here, there in parts:
-        xh1, dh1 = XH[here, :], F[here, :]
+        xh1 = jnp.concatenate([XH[0, here, 0:D // 2], XH[1, here, 0:D // 2]], 1).astype(f32)
+        dh1 = F[here, :]
         dr1 = ln_bwd(dh1, xh1, INV[here, 0:1], bias[10:11, :])
         DA[here, :] = dr1.astype(bf)
         sums = [s + fold(x) for s, x in zip(sums, (dh1 * xh1, dh1, dr1))]
@@ -216,26 +218,52 @@
         yield
 
 
-PER = 0.5
-
-
-def weave(main, side):
+def beside(main, side, count):
     credit = 0.0
-    for kind in main:
-        credit += PER * kind
+    for _ in range(8):
+        next(main)
+        credit += count / 8
         while credit >= 1:
             credit -= 1
             next(side, None)
-    for _ in side:
+
+
+def middle(i, tok, WO, WI, WT, bias, CTX, DC, DR, OB, G1, G2, G3, GB, AB, SLP, H1B, DB, DA, XH, F, INV):
+    tiles, sides = [], []
+    for u in range(2):
+        v = 1 - u
+        part = slice(u * R, (u + 1) * R)
+        tiles.append(tile(2 * i + u, tok, WO, WI, WT, bias, CTX, DC, DR, OB.at[:, part], GB, AB.at[u], SLP.at[u], H1B.at[u],
+                          DB.at[u], DA.at[u], XH.at[:, part], F.at[u], INV.at[u]))
+        sides.append(weights(jnp.maximum(2 * i + u - 1, 0), CTX, G1, G2, G3, GB, AB.at[v], SLP.at[v], H1B.at[v], DB.at[v], DA.at[v]))
+    (a, b), (before, between) = tiles, sides
+    beside(a, before, SPLIT)
+    for _ in range(4):
+        next(a)
+    beside(a, before, 11 - SPLIT)
+    for _ in before:
         pass
-
-
-def middle(i, tok, WO, WI, WT, bias, CTX, DC, DR, OB, G1, G2, G3, GB, AB, SLP, H1B, DB, DA, XH, F, INV):
-    for u in range(2):
-        now, last = 2 * i + u, jnp.maximum(2 * i + u - 1, 0)
-        v = 1 - u
-        weave(tile(now, tok, WO, WI, WT, bias, CTX, DC, DR, OB.at[:, u * R:(u + 1) * R], GB, AB.at[u], SLP.at[u], H1B.at[u], DB.at[u], DA.at[u], XH, F, INV),
-              weights(last, CTX, G1, G2, G3, GB, AB.at[v], SLP.at[v], H1B.at[v], DB.at[v], DA.at[v]))
+    for _ in range(4):
+        next(b)
+        next(a)
+        next(b)
+    for _ in range(4):
+        next(a)
+        next(b)
+        next(a)
+    for _ in a:
+        pass
+    beside(b, between, SPLIT)
+    for _ in range(4):
+        next(b)
+    beside(b, between, 11 - SPLIT)
+    for _ in between:
+        pass
+    for _ in b:
+        pass
+
+
+SPLIT = 5
 
 
 def qkv_grads(tok, Q, K, V, G1, GB):
@@ -466,10 +494,10 @@
     if remote:
         parts, refs = [refs[4 * k:4 * k + 4] for k in range(4)], refs[16:]
         RC, RU, Z, RV = parts
-    G1, G2, G3, GB, SC, AB, SLP, H1B, DB, DA, XH, F, INV, PB, in_sem, p_sem, o_sem, x_sem = refs[:18]
+    G1, G2, G3, GB, SC, AB, SLP, H1B, DB, DA, F, INV, PB, in_sem, p_sem, o_sem, x_sem = refs[:17]
     slots = tok.shape[0] // SL
     nmid = tok.shape[0] // (2 * R)
-    links = Links(cut, *refs[18:]) if remote else None
+    links = Links(cut, *refs[17:]) if remote else None
 
     def gather(stage, which):
         return sum((links.gather(stage, i, G[i]) for i in which), [])
@@ -555,7 +583,7 @@
     for u in range(UP):
         from_hbm(u, u).start()
 
-    OB = PB.at[2 * UP - 1]
+    OB, XH = PB.at[2 * UP - 1], PB.at[2 * UP - 2]
 
     def out_copy(i):
         return [pltpu.make_async_copy(OB.at[h, :, 0:D // 2], out.at[rows_of(i, 2 * R), h * (D // 2):(h + 1) * (D // 2)], o_sem.at[h])
@@ -670,8 +698,7 @@
         scratch += [vmem(u[1:] + s, bf) for u, s in back]
         scratch += [vmem((u[1] - 1,) + s, bf) for u, s in back]
     scratch += [vmem((GROUPS, GW, GU), f32)] * 2 + [vmem((D, D), f32), vmem((16, 8, D), f32), vmem((128, 128), f32)]
-    scratch += [vmem((2, GROUPS, R, GU), bf)] * 2 + [vmem((2, R, D), bf)] * 3 + [vmem((R, D), f32)] * 2
-    scratch += [vmem((R, 128), f32)]
+    scratch += [vmem((2, GROUPS, R, GU), bf)] * 2 + [vmem((2, R, D), bf)] * 3 + [vmem((2, R, D), f32), vmem((2, R, 128), f32)]
     scratch += [vmem((2 * cut.pairs, 2, SL, SL), bf), dma((2,)), dma((2 * cut.pairs,)), dma((2,)), dma((slots,))]
     params = dict(vmem_limit_bytes=64 * 1024 * 1024 - 65536)
     if remote:

time: 113 us -> 112 us (level)
    pallas_call x1, Pallas kernels: 108 us -> 107 us  [run_layer(): pl.pallas_call(functools.partial(layer, cut, remote), out_shape=(sd((rows...]
where the time goes in v5:
time: 112 us
  Pallas kernels  111 us (99%)
    pallas_call x1, Pallas kernels, run_layer(): pl.pallas_call(functools.partial(layer, cut, remote), out_shape=(sd((rows...  107 us
    pallas_call x1, Pallas kernels, run_finish(): pl.pallas_call(functools.partial(finish, cut), grid=(steps,), out_shape=t...  4.3 us

profile of v5, /device:TPU:0, one launch (start us, length us, event | category | flops | bytes accessed | tf_op | source)
XLA Modules:
  0.0 111.8 jit_solution(17023595006710055831)
XLA Ops:
  0.6 106.9 %shard_map.152 = (bf16[1536,768]{1,0:T(8,128)(2,1)}, bf16[1536,768]{1,0:T(8,128)(2,1)}, bf16[18,2,512,512]{3,2,1,0:T(8,128)(2,1)}, f32[24,384]{1,0:T(8,128)}, f3...) custom-call(s32[3]{0:T(128)} %length.1, bf16[72,192]{1,0:T(8,128)(2,1)} %refs_0_.1, ...), custom_call_target="tpu_custom_call" | custom-call | tf_op jit(solution)/shard_map/pallas_call | solution.py:708
  107.5 4.3 %shard_map.153 = (f32[72,192]{1,0:T(8,128)}, f32[4,24,192]{2,1,0:T(8,128)}, f32[4,24,192]{2,1,0:T(8,128)}, f32[10,24]{1,0:T(8,128)}, f32[2,24]{1,0:T(2,128)}, /*...) custom-call(f32[24,384]{1,0:T(8,128)} %get-tuple-element.22.qa, ...), custom_call_target="tpu_custom_call" | custom-call | tf_op jit(solution)/shard_map/pallas_call | solution.py:749

commit v6 on v5

--- a/solution.py
+++ b/solution.py
@@ -263,7 +263,7 @@
         pass
 
 
-SPLIT = 5
+SPLIT = 7
 
 
 def qkv_grads(tok, Q, K, V, G1, GB):
@@ -535,7 +535,8 @@
         arrive(gather(0, late))
         start(gather(1, late))
     loads[0].wait()
-    lax.fori_loop(0, slots, lambda s, x: (project(tok, WQ, SM, Q, K, V, s), x)[1], 0)
+    for s in range(slots):
+        project(tok, WQ, SM, Q, K, V, s)
 
     UP = cut.pairs
     steps = slots * PAIRS // UP
@@ -602,14 +603,19 @@
     for ref in (AB, SLP, H1B, DB, DA):
         ref[1] = jnp.zeros(ref.shape[1:], bf)
     lax.fori_loop(0, nmid, mid, 0)
-    for _ in weights(2 * nmid - 1, CTX, G1, G2, G3, GB, AB.at[1], SLP.at[1], H1B.at[1], DB.at[1], DA.at[1]):
+    if remote:
+        sent(sum((gather(stage, early + late) for stage in range(3)), []))
+    rest = weights(2 * nmid - 1, CTX, G1, G2, G3, GB, AB.at[1], SLP.at[1], H1B.at[1], DB.at[1], DA.at[1])
+    for _ in range(D // 256):
+        next(rest)
+    pack_o(cut, G3, G)
+    if remote:
+        start(scatter(0, (OW,)))
+    for _ in rest:
         pass
-    if remote:
-        sent(sum((gather(stage, early + late) for stage in range(3)), []))
-    pack_o(cut, G3, G)
     pack_f(cut, G1, G2, G)
     if remote:
-        start(scatter(0, late))
+        start(scatter(0, (FW,)))
 
     for copy in out_copy(nmid - 1):
         copy.wait()

time: 112 us -> 111 us (level)
  no operation moved by 1% of the time
where the time goes in v6:
time: 111 us
  Pallas kernels  110 us (99%)
    pallas_call x1, Pallas kernels, run_layer(): pl.pallas_call(functools.partial(layer, cut, remote), out_shape=(sd((rows...  106 us
    pallas_call x1, Pallas kernels, run_finish(): pl.pallas_call(functools.partial(finish, cut), grid=(steps,), out_shape=t...  4.3 us

profile of v6, /device:TPU:0, one launch (start us, length us, event | category | flops | bytes accessed | tf_op | source)
XLA Modules:
  0.0 111.1 jit_solution(6660749195338799633)
XLA Ops:
  0.6 106.1 %shard_map.152 = (bf16[1536,768]{1,0:T(8,128)(2,1)}, bf16[1536,768]{1,0:T(8,128)(2,1)}, bf16[18,2,512,512]{3,2,1,0:T(8,128)(2,1)}, f32[24,384]{1,0:T(8,128)}, f3...) custom-call(s32[3]{0:T(128)} %length.1, bf16[72,192]{1,0:T(8,128)(2,1)} %refs_0_.1, ...), custom_call_target="tpu_custom_call" | custom-call | tf_op jit(solution)/shard_map/pallas_call | solution.py:714
  106.8 4.3 %shard_map.153 = (f32[72,192]{1,0:T(8,128)}, f32[4,24,192]{2,1,0:T(8,128)}, f32[4,24,192]{2,1,0:T(8,128)}, f32[10,24]{1,0:T(8,128)}, f32[2,24]{1,0:T(2,128)}, /*...) custom-call(f32[24,384]{1,0:T(8,128)} %get-tuple-element.22.qa, ...), custom_call_target="tpu_custom_call" | custom-call | tf_op jit(solution)/shard_map/pallas_call | solution.py:755
